TPU v7x, 512 devices: a whole 4x4x16 slice. The times are simulated.
512 devices in a mesh: clus: 16 (over z_lo, x), dir: 32 (over y, z_hi, core).
Axes of the slice: x: 4, y: 4, z: 16 (z_hi: 4, z_lo: 4; z = z_hi * 4 + z_lo), core: 2. Of those that a mesh axis runs over, the one named last changes fastest.
Arguments:
- child_patterns: float32 [768, 2, 256, 128], P('clus', None, 'dir'), may hold values from -6 to 6
- trans_table: bfloat16 [316, 2, 73728], P(None, None, 'dir'), may hold values from -0.875 to 0.875
- child_parent: int32 [16, 48], P('clus'), may hold values from 0 to 7, never falling along the last dimension, each value on 1 to 8 neighbouring positions
- child_octant: int32 [768], P('clus'), may hold values from 0 to 7
- partner_src: int32 [128, 56], replicated, may hold values from 0 to 127, as said below
- partner_off: int32 [128, 56], replicated, may hold values from 0 to 315
- partner_count: int32 [128], replicated, may hold values from 15 to 56, as said below
Outputs:
- child_incoming: float32 [768, 2, 256, 128], P('clus', None, 'dir')
Inputs may be any that keep to these rules, and one draw needn't show every extreme that they name: `partner_src`: each row lists 56 distinct parent clusters, none equal to the row's own index. `partner_count`: the number of live slots at the head of each row of partner_src and partner_off. On one index of clus, all of its 8 parents have 56 live slots. `child_parent`: Non-decreasing along each row; every one of the 8 parents of the row has 1 to 8 children.
All inputs are finite; a program needn't handle non-finite values.
Results may differ from a plain program's by a relative error of at most 0.0003.
Values sent between devices are 32-bit elements; how exact they have to be, the bound alone decides.
A program may use at most 64 MiB of HBM per device.

v0:
```python
import math

import jax
import jax.numpy as jnp
from jax import lax
from jax.sharding import PartitionSpec as P

NTHETA_C = 128
NPHI_C = 256
NTHETA_P = 192
NPHI_P = 384


phase_scale = 8.0 * math.pi
highest = lax.Precision.HIGHEST


def with_halo(shard, sides, width):
    for axis, dim in sides:
        size, length = (lax.axis_size(axis), shard.shape[dim])
        up = [(i, (i + 1) % size) for i in range(size)]
        down = [(j, i) for i, j in up]
        last = lax.slice_in_dim(shard, length - width, length, axis=dim)
        initial = lax.slice_in_dim(shard, 0, width, axis=dim)
        before = lax.ppermute(last, axis, up)
        after = lax.ppermute(initial, axis, down)
        shard = jnp.concatenate([before, shard, after], axis=dim)
    return shard


def lagrange(offset):
    weights = []
    for anchor in range(5):
        factor = jnp.ones_like(offset)
        for neighbour in range(5):
            if neighbour != anchor:
                factor = factor * (offset - neighbour) / (anchor - neighbour)
        weights.append(factor)
    return weights


def polar_matrix_of(rows_out, rows_in):
    target = (jnp.arange(rows_out, dtype=jnp.float32) + 0.5) * rows_in / rows_out - 0.5
    start_row = jnp.clip(jnp.floor(target + 0.5).astype(jnp.int32) - 2, 0, rows_in - 5)
    weights = lagrange(target - start_row.astype(jnp.float32))
    columns = jnp.arange(rows_in, dtype=jnp.int32)
    matrix = jnp.zeros((rows_out, rows_in), jnp.float32)
    for anchor in range(5):
        matrix = matrix + jnp.where(
            columns[None, :] == (start_row + anchor)[:, None], weights[anchor][:, None], 0.0
        )
    return matrix


def azimuth_matrix_of(out_index, in_index, total_out, total_in):
    target = (out_index * total_in).astype(jnp.float32) / total_out
    nearest = jnp.floor(target + 0.5).astype(jnp.int32)
    weights = lagrange(target - nearest.astype(jnp.float32) + 2.0)
    matrix = jnp.zeros((out_index.shape[0], in_index.shape[0]), jnp.float32)
    for anchor in range(5):
        columns = nearest + anchor - 2
        matrix = matrix + jnp.where(
            in_index[None, :] == columns[:, None], weights[anchor][:, None], 0.0
        )
    return matrix


def shift_phases(octant, azimuth_index, azimuth_total, polar_total):
    azimuth = 2.0 * math.pi * azimuth_index.astype(jnp.float32) / azimuth_total
    polar = math.pi * (jnp.arange(polar_total, dtype=jnp.float32) + 0.5) / polar_total
    first_axis = jnp.sin(polar)[None, :] * jnp.cos(azimuth)[:, None]
    second_axis = jnp.sin(polar)[None, :] * jnp.sin(azimuth)[:, None]
    third_axis = jnp.cos(polar)[None, :] * jnp.ones_like(azimuth)[:, None]
    first_sign = (1 - 2 * (octant % 2)).astype(jnp.float32)
    second_sign = (1 - 2 * (octant // 2 % 2)).astype(jnp.float32)
    third_sign = (1 - 2 * (octant // 4)).astype(jnp.float32)
    phase_angle = phase_scale * (
        first_sign[:, None, None] * first_axis[None]
        + second_sign[:, None, None] * second_axis[None]
        + third_sign[:, None, None] * third_axis[None]
    )
    return (jnp.cos(phase_angle), jnp.sin(phase_angle))


def translate(sources, table, partner_src, partner_off, partner_count):
    live_mask = (
        jnp.arange(partner_src.shape[1], dtype=jnp.int32)[None, :] < partner_count[:, None]
    ).astype(jnp.float32)
    picked = sources[partner_src]
    operator = table[partner_off].astype(jnp.float32) * live_mask[:, :, None, None]
    real_part = jnp.sum(
        operator[:, :, 0] * picked[:, :, 0] - operator[:, :, 1] * picked[:, :, 1], axis=1
    )
    imaginary = jnp.sum(
        operator[:, :, 0] * picked[:, :, 1] + operator[:, :, 1] * picked[:, :, 0], axis=1
    )
    return jnp.stack([real_part, imaginary], axis=1)


def forward_shift(patterns, cosine, sine_part):
    real_part = patterns[:, 0] * cosine - patterns[:, 1] * sine_part
    imaginary = patterns[:, 0] * sine_part + patterns[:, 1] * cosine
    return jnp.stack([real_part, imaginary], axis=1)


def conjugate_shift(patterns, cosine, sine_part):
    real_part = patterns[:, 0] * cosine + patterns[:, 1] * sine_part
    imaginary = patterns[:, 1] * cosine - patterns[:, 0] * sine_part
    return jnp.stack([real_part, imaginary], axis=1)


def on_device(
    child_patterns, trans_table, child_parent, child_octant, partner_src, partner_off, partner_count
):
    child_slots, _, azimuth_in, polar_in = child_patterns.shape
    polar_out = NTHETA_P
    azimuth_out = trans_table.shape[2] // polar_out
    parent_slots = partner_src.shape[0] // lax.axis_size("clus")
    cluster_index = lax.axis_index("clus")
    direction_index = lax.axis_index("dir")
    parents = child_parent[0]
    polar_matrix = polar_matrix_of(NTHETA_P, NTHETA_C)
    onehot = (parents[None, :] == jnp.arange(parent_slots, dtype=jnp.int32)[:, None]).astype(
        jnp.float32
    )
    own_rows = jnp.mod(
        direction_index * azimuth_out + jnp.arange(azimuth_out, dtype=jnp.int32), NPHI_P
    )
    cosine, sine_part = shift_phases(child_octant, own_rows, NPHI_P, polar_out)
    extended = with_halo(child_patterns, (("dir", 2),), 2)
    gather_matrix = azimuth_matrix_of(
        jnp.arange(azimuth_out, dtype=jnp.int32),
        jnp.arange(azimuth_in + 4, dtype=jnp.int32) - 2,
        NPHI_P,
        NPHI_C,
    )
    along_azimuth = jnp.einsum("pc,kacz->kapz", gather_matrix, extended, precision=highest)
    refined = jnp.einsum("kapz,tz->kapt", along_azimuth, polar_matrix, precision=highest)
    shifted = forward_shift(refined, cosine, sine_part)
    radiation = jnp.einsum("gk,kapt->gapt", onehot, shifted, precision=highest)
    flattened = radiation.reshape(parent_slots, 2, azimuth_out * polar_out)
    sources = lax.all_gather(flattened, "clus", axis=0, tiled=True)
    first_row = cluster_index * parent_slots
    own_src = lax.dynamic_slice_in_dim(partner_src, first_row, parent_slots, 0)
    own_off = lax.dynamic_slice_in_dim(partner_off, first_row, parent_slots, 0)
    own_count = lax.dynamic_slice_in_dim(partner_count, first_row, parent_slots, 0)
    incoming = translate(sources, trans_table, own_src, own_off, own_count)
    incoming = incoming.reshape(parent_slots, 2, azimuth_out, polar_out)
    return_matrix = azimuth_matrix_of(
        jnp.arange(azimuth_out + 6, dtype=jnp.int32) - 3,
        jnp.arange(azimuth_in, dtype=jnp.int32),
        NPHI_P,
        NPHI_C,
    )
    per_child = jnp.einsum("gk,gapt->kapt", onehot, incoming, precision=highest)
    returned = conjugate_shift(per_child, cosine, sine_part)
    coarse_own = jnp.einsum("kapt,tz->kapz", returned, polar_matrix, precision=highest)
    coarse = with_halo(coarse_own, (("dir", 2),), 3)
    return jnp.einsum("pc,kapz->kacz", return_matrix, coarse, precision=highest)


def solution(mesh):
    return jax.shard_map(
        on_device,
        mesh=mesh,
        in_specs=(
            P("clus", None, "dir", None),
            P(None, None, "dir"),
            P("clus", None),
            P("clus"),
            P(),
            P(),
            P(),
        ),
        out_specs=P("clus", None, "dir", None),
        check_vma=False,
    )
```

profile of v0, /device:TPU:1, one launch (start us, length us, event | category | flops | bytes accessed | tf_op | source)
XLA Modules:
  0.0 204.2 jit_solution(9964516812942284886)
XLA Ops:
  6.5 1.3 fusion.124
  7.9 10.3 %collective-permute-start = (f32[48,2,2,128]{3,2,1,0:T(2,128)S(1)}, f32[48,2,2,128]{3,2,1,0:T(2,128)S(1)}, u32[]{:S(2)}, u32[]{:S(2)}) collective-permute-start(f32[48,2,2,128]{3,2,1,0:T(2,128)S(1)} %get-tuple-element.13), channel_id=1, source_target_pairs={{0,1},{1,2},{2,3},{3,4},{4,5},{5,6},{6,7},{7,8},{8,9},{9,10},{10,1... | collective-permute-start | bytes 294920 | tf_op jit(solution)/shard_map/ppermute | solution.py:25
  18.3 1.9 collective-permute-start.1
  20.6 0.7 fusion.106
  21.3 6.8 %collective-permute-done.1 = f32[48,2,2,128]{3,2,1,0:T(2,128)S(1)} collective-permute-done((f32[48,2,2,128]{3,2,1,0:T(2,128)S(1)}, f32[48,2,2,128]{3,2,1,0:T(2,128)S(1)}, u32[]{:S(2)}, u32[]{:S(2)}) %collective-permute-start.1) | collective-permute-done | bytes 98336 | tf_op jit(solution)/shard_map/ppermute | solution.py:26
  28.1 2.0 convolution_bitcast_fusion
  30.1 1.5 fusion.14
  31.7 2.6 %multiply_subtract_fusion.1 = (f32[48,1,12,192]{3,0,2,1:T(8,128)S(1)}, f32[48,1,12,192]{3,0,2,1:T(8,128)S(1)}) fusion(f32[48,2,12,192]{3,0,2,1:T(8,128)S(1)} %fusion.14, f32[192]{0:T(256)S(1)} %fusion.102, f32[48]{0:T(128)S(1)} %get-tuple-element.19, f32[12,192]{1,0:T(8,128)S(1)} %get-tuple-element.16, f32[48]{0:T(128)S(1)} %get-tuple-element.18, ...), kind=kLoop, calls=%fused_computation.27 | loop fusion | flops 1327104 | bytes 1789248 | tf_op jit(solution)/shard_map/sub | solution.py:101
  34.3 0.5 fusion
  34.9 0.8 reshape.383
  36.3 20.4 %gather_fusion = bf16[448,2,2304]{2,1,0:T(2,128)(2,1)} fusion(bf16[316,2,2304]{2,1,0:T(2,128)(2,1)S(1)} %copy-done, s32[1024]{0:T(1024)S(1)} %pad_clamp_fusion.1), kind=kCustom, calls=%fused_computation | custom fusion | bytes 8259328 | tf_op jit(solution)/shard_map/gather | solution.py:90
  56.8 8.4 %convert_multiply_fusion = f32[8,56,2,2304]{3,2,1,0:T(2,128)} fusion(bf16[8,56,2,2304]{3,2,1,0:T(2,128)(2,1)} %bitcast.32, f32[8,56]{1,0:T(8,128)S(1)} %fusion.86), kind=kLoop, calls=%fused_computation.2 | loop fusion | flops 4128768 | bytes 12388096 | tf_op jit(solution)/shard_map/mul | solution.py:90
  65.2 53.1 %all-gather.2.cloned.1.call-done = f32[128,2,2304]{2,1,0:T(2,128)} async-done(((f32[8,2,2304]{2,1,0:T(2,128)}), f32[128,2,2304]{2,1,0:T(2,128)}) %all-gather.2.cloned.1.call-update) | async-done | bytes 2359312 | tf_op jit(solution)/shard_map/all_gather | solution.py:142
  118.2 22.7 %gather_fusion.1 = f32[448,2,2304]{2,1,0:T(2,128)} fusion(f32[128,2,2304]{2,1,0:T(2,128)} %all-gather.2.cloned.1.call-done, s32[1024]{0:T(1024)S(1)} %pad_clamp_fusion), kind=kCustom, calls=%fused_computation.1 | custom fusion | bytes 16516864 | tf_op jit(solution)/shard_map/gather | solution.py:89
  140.9 22.2 %subtract_reduce_fusion = (f32[8,2304]{1,0:T(8,128)S(1)}, f32[8,2304]{1,0:T(8,128)S(1)}) fusion(f32[8,56,2,2304]{3,2,1,0:T(2,128)} %bitcast.31, f32[8,56,2,2304]{3,2,1,0:T(2,128)} %convert_multiply_fusion), kind=kLoop, calls=%fused_computation.4 | loop fusion | flops 8220672 | bytes 16662528 | tf_op jit(solution)/shard_map/reduce_sum | solution.py:91
  163.1 0.1 stack.20
  163.5 0.7 fusion.18
  164.1 2.4 %multiply_add_fusion = (f32[48,1,12,192]{3,0,2,1:T(8,128)S(1)}, f32[48,1,12,192]{3,0,2,1:T(8,128)S(1)}) fusion(f32[48,2,12,192]{3,0,2,1:T(8,128)S(1)} %fusion.18, f32[192]{0:T(256)S(1)} %fusion.102, f32[48]{0:T(128)S(1)} %get-tuple-element.19, f32[12,192]{1,0:T(8,128)S(1)} %get-tuple-element.16, f32[48]{0:T(128)S(1)} %get-tuple-element.18, ...), kind=kLoop, calls=%fused_computation.25 | loop fusion | flops 1327104 | bytes 1789248 | tf_op jit(solution)/shard_map/add | solution.py:107
  166.6 1.4 fusion.4
  168.0 16.7 %collective-permute-start.2 = (f32[48,2,3,128]{3,0,2,1:T(8,128)S(1)}, f32[48,2,3,128]{3,0,2,1:T(8,128)S(1)}, u32[]{:S(2)}, u32[]{:S(2)}) collective-permute-start(f32[48,2,3,128]{3,0,2,1:T(8,128)S(1)} %get-tuple-element.11), channel_id=1, source_target_pairs={{0,1},{1,2},{2,3},{3,4},{4,5},{5,6},{6,7},{7,8},{8,9},{9,10},{10,1... | collective-permute-start | bytes 442376 | tf_op jit(solution)/shard_map/ppermute | solution.py:25
  184.7 1.9 collective-permute-start.3
  186.7 0.1 collective-permute-done.2
  186.8 8.7 %collective-permute-done.3 = f32[48,2,3,128]{3,0,2,1:T(8,128)S(1)} collective-permute-done((f32[48,2,3,128]{3,0,2,1:T(8,128)S(1)}, f32[48,2,3,128]{3,0,2,1:T(8,128)S(1)}, u32[]{:S(2)}, u32[]{:S(2)}) %collective-permute-start.3) | collective-permute-done | bytes 147488 | tf_op jit(solution)/shard_map/ppermute | solution.py:26
  195.6 1.8 convolution_bitcast_fusion.1
  (49 shorter events, 1.5 us)
Async XLA Ops:
  6.5 29.7 %copy-start = (bf16[316,2,2304]{2,1,0:T(2,128)(2,1)S(1)}, bf16[316,2,2304]{2,1,0:T(2,128)(2,1)}, u32[]{:S(2)}) copy-start(bf16[316,2,2304]{2,1,0:T(2,128)(2,1)} %param.8) | copy-start | bytes 8736772
  6.5 27.7 %copy-start.3 = (s32[1,48]{1,0:T(1,128)S(1)}, s32[1,48]{1,0:T(1,128)}, u32[]{:S(2)}) copy-start(s32[1,48]{1,0:T(1,128)} %param.9) | copy-start | bytes 580
  6.5 111.7 %all-gather.2.cloned.1.call-start = ((), (), s32[]{:S(2)}) async-start(), calls=%async_computation | async-start | bytes 2506752 | tf_op jit(solution)/shard_map/all_gather | solution.py:142
  7.9 27.9 %copy-start.4 = (s32[128]{0:T(128)S(1)}, s32[128]{0:T(128)}, u32[]{:S(2)}) copy-start(s32[128]{0:T(128)} %param.13) | copy-start | bytes 1540
  7.9 27.9 %copy-start.1 = (s32[128,56]{0,1:T(8,128)S(1)}, s32[128,56]{0,1:T(8,128)}, u32[]{:S(2)}) copy-start(s32[128,56]{0,1:T(8,128)} %param.11) | copy-start | bytes 86020
  7.9 27.9 %copy-start.2 = (s32[128,56]{0,1:T(8,128)S(1)}, s32[128,56]{0,1:T(8,128)}, u32[]{:S(2)}) copy-start(s32[128,56]{0,1:T(8,128)} %param.12) | copy-start | bytes 86020
  7.9 13.4 %collective-permute-start = (f32[48,2,2,128]{3,2,1,0:T(2,128)S(1)}, f32[48,2,2,128]{3,2,1,0:T(2,128)S(1)}, u32[]{:S(2)}, u32[]{:S(2)}) collective-permute-start(f32[48,2,2,128]{3,2,1,0:T(2,128)S(1)} %get-tuple-element.13), channel_id=1, source_target_pairs={{0,1},{1,2},{2,3},{3,4},{4,5},{5,6},{6,7},{7,8},{8,9},{9,10},{10,1... | collective-permute-start | bytes 294920 | tf_op jit(solution)/shard_map/ppermute | solution.py:25
  18.3 9.9 %collective-permute-start.1 = (f32[48,2,2,128]{3,2,1,0:T(2,128)S(1)}, f32[48,2,2,128]{3,2,1,0:T(2,128)S(1)}, u32[]{:S(2)}, u32[]{:S(2)}) collective-permute-start(f32[48,2,2,128]{3,2,1,0:T(2,128)S(1)} %get-tuple-element.14), channel_id=1, source_target_pairs={{1,0},{2,1},{3,2},{4,3},{5,4},{6,5},{7,6},{8,7},{9,8},{10,9},{11,1... | collective-permute-start | bytes 294920 | tf_op jit(solution)/shard_map/ppermute | solution.py:26
  168.0 18.8 %collective-permute-start.2 = (f32[48,2,3,128]{3,0,2,1:T(8,128)S(1)}, f32[48,2,3,128]{3,0,2,1:T(8,128)S(1)}, u32[]{:S(2)}, u32[]{:S(2)}) collective-permute-start(f32[48,2,3,128]{3,0,2,1:T(8,128)S(1)} %get-tuple-element.11), channel_id=1, source_target_pairs={{0,1},{1,2},{2,3},{3,4},{4,5},{5,6},{6,7},{7,8},{8,9},{9,10},{10,1... | collective-permute-start | bytes 442376 | tf_op jit(solution)/shard_map/ppermute | solution.py:25
  184.7 10.8 %collective-permute-start.3 = (f32[48,2,3,128]{3,0,2,1:T(8,128)S(1)}, f32[48,2,3,128]{3,0,2,1:T(8,128)S(1)}, u32[]{:S(2)}, u32[]{:S(2)}) collective-permute-start(f32[48,2,3,128]{3,0,2,1:T(8,128)S(1)} %get-tuple-element.12), channel_id=1, source_target_pairs={{1,0},{2,1},{3,2},{4,3},{5,4},{6,5},{7,6},{8,7},{9,8},{10,9},{11,1... | collective-permute-start | bytes 442376 | tf_op jit(solution)/shard_map/ppermute | solution.py:26
Sparse Core Ops, SparseCore 0:
  35.9 82.3 all-gather.1
where the time goes:
time: 205 us; the launch traced here: 204 us
  waiting for transfers between devices  68.7 us (34%)
  local copies, waits for them, and re-layouts  46 us (22%)
  other arithmetic  37.1 us (18%)
  starting transfers between devices  30.9 us (15%)
  between operations  13.6 us (7%)
  matrix products  7.91 us (4%)
    all_gather x1, waiting for transfers between devices, on_device(): sources = lax.all_gather(flattened, 'clus', axis=0, tiled=True)  53.1 us
    ppermute x2, starting transfers between devices, with_halo(): before = lax.ppermute(last, axis, up)  27 us
    gather x1, local copies, waits for them, and re-layouts, translate(): picked = sources[partner_src]  22.7 us
    reduce_sum x1, other arithmetic, translate(): jnp.sum(operator[:, :, 0] * picked[:, :, 0] - operator[:, :, 1] * picked[...  22.2 us
    gather x1, local copies, waits for them, and re-layouts, translate(): table[partner_off].astype(jnp.float32) * live_mask[:, :, None, None]  20.4 us
    ppermute x2, waiting for transfers between devices, with_halo(): after = lax.ppermute(initial, axis, down)  15.5 us
    mul x1, other arithmetic, translate(): table[partner_off].astype(jnp.float32) * live_mask[:, :, None, None]  8.36 us
  transfers between devices with their start and end apart: 5, of which 4 were waited for; matrix products, arithmetic and copies ran while one was open for 15% of the time, Pallas kernels for 0%

commit v1 on v0

v1 whole, which is shorter than its diff:
```python
import functools
import math

import jax
import jax.numpy as jnp
import ml_dtypes
import numpy as np
from jax import lax
from jax.experimental import pallas as pl
from jax.experimental.pallas import tpu as pltpu
from jax.sharding import PartitionSpec as P

NT_C, NP_C, NT_P, NP_P = 128, 256, 192, 384
OFFSETS = 316
N_CLUS, N_DIR = 16, 32
PAR, KIDS = 8, 48
TILES = PAR * 6
ROWS = 6 * TILES
PAD = OFFSETS * 32
MESH = pl.DeviceIdType.MESH
EVEN = np.array([-2, 0, 2, 4, 6, 8, 10, 14])
ODD = np.array([-1, 1, 3, 5, 7, 9, 11, 13])


def lagrange(t):
    out = []
    for m in range(5):
        w = np.ones_like(t)
        for n in range(5):
            if n != m:
                w = w * (t - n) / (m - n)
        out.append(w)
    return out


def polar_matrix():
    x = (np.arange(NT_P) + 0.5) * NT_C / NT_P - 0.5
    s = np.clip(np.floor(x + 0.5).astype(int) - 2, 0, NT_C - 5)
    w = lagrange(x - s)
    m = np.zeros((NT_P, NT_C))
    for k in range(5):
        m[np.arange(NT_P), s + k] = w[k]
    return m


def azimuth_rows(rows):
    x = rows * NP_C / NP_P
    b = np.floor(x + 0.5).astype(int)
    w = lagrange(x - b + 2)
    m = np.zeros((len(rows), 8))
    for k in range(5):
        for j in range(len(rows)):
            i = b[j] + k - 2
            if 0 <= i < 8:
                m[j, i] = w[k][j]
    return m


def halves(a):
    a = a.astype(np.float32)
    hi = a.astype(ml_dtypes.bfloat16)
    lo = (a - hi.astype(np.float32)).astype(ml_dtypes.bfloat16)
    return np.stack([hi, lo])


def in_tiles(even, odd):
    return np.stack([even[:, :128], np.concatenate([even[:, 128:], odd[:, :64]], 1), odd[:, 64:]])


@functools.cache
def constants():
    p = polar_matrix()
    ae, ao = azimuth_rows(EVEN), azimuth_rows(ODD)
    eye = np.eye(16)
    up_left = halves(np.concatenate([np.kron(eye, ae), np.kron(eye, ao)], 0))
    w = np.zeros((256, 384))
    w[:128, :192] = p.T
    w[128:, 192:] = p.T
    up_right = halves(w)
    down_right = halves(np.stack([w[:128, :256].T, w[128:, 128:].T]))
    down_left = halves(np.concatenate([np.kron(eye, ae.T), np.kron(eye, ao.T)], 1))
    theta = math.pi * (np.arange(NT_P) + 0.5) / NT_P
    phases = np.zeros((N_DIR, 3, 2, 3, 8, 128))
    for d in range(N_DIR):
        angle = []
        for rows in (EVEN, ODD):
            phi = 2 * math.pi * ((12 * d + rows) % NP_P) / NP_P
            angle.append(
                8 * math.pi
                * np.stack(
                    [
                        np.sin(theta) * np.cos(phi)[:, None],
                        np.sin(theta) * np.sin(phi)[:, None],
                        np.cos(theta) * np.ones((8, 1)),
                    ]
                )
            )
        for k in range(3):
            t = in_tiles(angle[0][k], angle[1][k])
            phases[d, k] = np.stack([np.cos(t), np.sin(t)])
    return up_left, up_right, down_right, down_left, phases.reshape(N_DIR, 144, 128).astype(np.float32)


def split(x):
    hi = x.astype(jnp.bfloat16)
    return hi, (x - hi.astype(jnp.float32)).astype(jnp.bfloat16)


def dot3(a, b):
    f = functools.partial(jnp.dot, preferred_element_type=jnp.float32)
    return f(a[0], b[0]) + (f(a[1], b[0]) + f(a[0], b[1]))


def position():
    clus, direction = lax.axis_index("clus"), lax.axis_index("dir")
    core = lax.rem(direction, 2)
    x, z = lax.rem(clus, 4), lax.div(clus, 4)
    return clus, direction, core, x, z


def gather_member(core, x, z, k):
    return (1 - core) * (z * 4 + k) + core * (k * 4 + x)


def reduce_member(core, x, z, k):
    return (1 - core) * (k * 4 + x) + core * (z * 4 + k)


def octant_tables(base, table):
    def tile(k, a, c):
        r = (k * 6 + a * 3 + c) * 8
        return base[r : r + 8, :]

    for c in range(3):
        ar, ai, br, bi, cr, ci = (tile(k, a, c) for k in range(3) for a in range(2))
        rr, ii, ri, ir = ar * br, ai * bi, ar * bi, ai * br
        for sx, sy, re, im in ((1, 1, rr - ii, ri + ir), (1, -1, rr + ii, ir - ri)):
            pr, pi, qr, qi = re * cr, im * ci, re * ci, im * cr
            for sz, fr, fi in ((1, pr - pi, qr + qi), (-1, pr + pi, qi - qr)):
                for sign in (1, -1):
                    o = (sx * sign < 0) + 2 * (sy * sign < 0) + 4 * (sz * sign < 0)
                    table[(o * 6 + c) * 8 : (o * 6 + c) * 8 + 8, :] = fr
                    table[(o * 6 + 3 + c) * 8 : (o * 6 + 3 + c) * 8 + 8, :] = fi if sign > 0 else -fi


def build_lists(src_ref, off_ref, count_ref, key_ref, list_ref):
    clus, direction, core, x, z = position()
    lane8 = lax.broadcasted_iota(jnp.int32, (8, 128), 1)
    sub8 = lax.broadcasted_iota(jnp.int32, (8, 128), 0)
    keys, sums = [], []
    key_ref[...] = jnp.full((32, 128), PAD, jnp.int32)
    for k in range(4):
        first = pl.multiple_of(8 * reduce_member(core, x, z, k), 8)
        counts = jnp.sum(
            jnp.where(lane8 == first + sub8, count_ref[...], 0), axis=1, keepdims=True
        )
        src = src_ref[pl.ds(first, 8), :]
        off = off_ref[pl.ds(first, 8), :]
        slot = lax.broadcasted_iota(jnp.int32, src.shape, 1)
        owner = src >> 3
        own_x, own_z = owner & 3, owner >> 2
        here = jnp.where(core == 0, own_z, own_x) == jnp.where(core == 0, z, x)
        where_from = jnp.where(core == 0, own_x, own_z) * 8 + (src & 7)
        live = here & (slot < counts)
        key_ref[8 * k : 8 * k + 8, 0 : src.shape[1]] = jnp.where(live, off * 32 + where_from, PAD)
    key = key_ref[...]
    lane = lax.broadcasted_iota(jnp.int32, (32, 128), 1)
    number = jnp.sum((key < PAD).astype(jnp.int32), axis=1, keepdims=True)
    size = 2
    while size <= 64:
        j = size // 2
        while j >= 1:
            low = (lane & j) == 0
            other = jnp.where(low, pltpu.roll(key, 128 - j, 1), pltpu.roll(key, j, 1))
            take_min = low == ((lane & size) == 0)
            key = jnp.where(take_min, jnp.minimum(key, other), jnp.maximum(key, other))
            j //= 2
        size *= 2
    list_ref[...] = jnp.where(lane < 64, key, number)


def aggregate_kernel(
    parent_ref, octant_ref, child_ref, src_ref, off_ref, count_ref, left_ref, right_ref, phases_ref,
    part_ref, list_ref, z_ref, base_ref, table_ref, acc_ref, key_ref, sem,
):
    copy = pltpu.make_async_copy(phases_ref.at[lax.axis_index("dir")], base_ref, sem)
    copy.start()
    build_lists(src_ref, off_ref, count_ref, key_ref, list_ref)
    for n in range(6):
        x = split(child_ref[8 * n : 8 * n + 8].reshape(128, 128))
        eo = dot3((left_ref[0], left_ref[1]), x)
        y = split(jnp.concatenate([eo[:128], eo[128:]], axis=1))
        z_ref[128 * n : 128 * n + 128, :] = dot3(y, (right_ref[0], right_ref[1]))
    copy.wait()
    octant_tables(base_ref, table_ref)

    def child(k, acc):
        parent = parent_ref[0, k]
        before = parent_ref[0, jnp.maximum(k - 1, 0)]
        keep = jnp.where((parent == before) & (k > 0), 1.0, 0.0)
        o = octant_ref[k]
        new = []
        for c in range(3):
            re = z_ref[pl.ds(pl.multiple_of(k * 16, 8), 8), 128 * c : 128 * c + 128]
            im = z_ref[pl.ds(pl.multiple_of(k * 16 + 8, 8), 8), 128 * c : 128 * c + 128]
            fr = table_ref[pl.ds(pl.multiple_of((o * 6 + c) * 8, 8), 8), :]
            fi = table_ref[pl.ds(pl.multiple_of((o * 6 + 3 + c) * 8, 8), 8), :]
            new.append(acc[c] * keep + (re * fr - im * fi))
            new.append(acc[3 + c] * keep + (re * fi + im * fr))
        new = new[0::2] + new[1::2]
        for t in range(6):
            acc_ref[pl.ds(pl.multiple_of((parent * 6 + t) * 8, 8), 8), :] = new[t]
        return tuple(new)

    lax.fori_loop(0, KIDS, child, tuple(jnp.zeros((8, 128), jnp.float32) for _ in range(6)), unroll=4)
    for s in range(8):
        part_ref[s * TILES : (s + 1) * TILES, :] = acc_ref[pl.ds(s, TILES, stride=8), :]


def enter(peers):
    barrier = pltpu.get_barrier_semaphore()
    for peer in peers:
        pl.semaphore_signal(barrier, inc=1, device_id=peer, device_id_type=MESH)
    pl.semaphore_wait(barrier, len(peers))


def even_lanes():
    column = lax.rem(lax.broadcasted_iota(jnp.int32, (TILES, 128), 0), 3)
    lane = lax.broadcasted_iota(jnp.int32, (TILES, 128), 1)
    return (column == 0) | ((column == 1) & (lane < 64))


def gather_kernel(part_ref, out_ref, halo_ref, send_sem, recv_sem):
    clus, direction, core, x, z = position()
    after = (clus, lax.rem(direction + 1, N_DIR))
    before = (clus, lax.rem(direction + N_DIR - 1, N_DIR))
    me = (1 - core) * x + core * z
    peers = [(gather_member(core, x, z, lax.rem(me + r, 4)), direction) for r in (1, 2, 3)]
    enter([after, before, *peers])
    forward = pltpu.make_async_remote_copy(
        part_ref.at[pl.ds(7 * TILES, TILES)], halo_ref.at[0], send_sem.at[0], recv_sem.at[0],
        device_id=after, device_id_type=MESH,
    )
    backward = pltpu.make_async_remote_copy(
        part_ref.at[pl.ds(0, TILES)], halo_ref.at[1], send_sem.at[1], recv_sem.at[1],
        device_id=before, device_id_type=MESH,
    )
    forward.start()
    backward.start()
    own = pl.multiple_of(me * ROWS, 8)
    out_ref[pl.ds(own, ROWS), :] = part_ref[TILES : TILES + ROWS, :]
    forward.wait_recv()
    even = even_lanes()
    got = halo_ref[0]
    q0 = pl.ds(pl.multiple_of(own, 8), TILES)
    q1 = pl.ds(pl.multiple_of(own + TILES, 8), TILES)
    q5 = pl.ds(pl.multiple_of(own + 5 * TILES, 8), TILES)
    out_ref[q0, :] += jnp.where(even, 0.0, got)
    out_ref[q1, :] += jnp.where(even, got, 0.0)
    backward.wait_recv()
    out_ref[q5, :] += halo_ref[1]
    copies = []
    for r, peer in enumerate(peers):
        block = out_ref.at[pl.ds(own, ROWS)]
        copy = pltpu.make_async_remote_copy(
            block, block, send_sem.at[2 + r], recv_sem.at[2 + r], device_id=peer, device_id_type=MESH
        )
        copy.start()
        copies.append(copy)
    for copy in copies:
        copy.wait()
    forward.wait_send()
    backward.wait_send()


def translate_kernel(list_ref, table_in, s_ref, out_ref, table_ref):
    rows = table_in.shape[0]
    step = 144

    def widen(i, carry):
        at = pl.ds(pl.multiple_of(i * step, 16), step)
        table_ref[at, :] = table_in[at, :].astype(jnp.float32)
        return carry

    lax.fori_loop(0, rows // step, widen, 0)
    table_ref[rows : rows + 40, :] = jnp.zeros((40, 128), jnp.float32)

    def target(t, carry):
        def four(b, acc):
            acc = list(acc)
            for u in range(4):
                code = list_ref[t, b * 4 + u]
                o, s = code >> 5, code & 31
                trow = o * 36
                srow = (s >> 3) * ROWS + (s & 7) * 6
                for c in range(3):
                    tr = table_ref[pl.ds(trow + 2 * c, 6, stride=6), :]
                    ti = table_ref[pl.ds(trow + 2 * c + 1, 6, stride=6), :]
                    sr = s_ref[pl.ds(srow + c, 6, stride=TILES), :]
                    si = s_ref[pl.ds(srow + 3 + c, 6, stride=TILES), :]
                    acc[c] = acc[c] + (tr * sr - ti * si)
                    acc[3 + c] = acc[3 + c] + (tr * si + ti * sr)
            return tuple(acc)

        number = list_ref[t, 64]
        zero = jnp.zeros((6, 128), jnp.float32)
        acc = lax.fori_loop(0, (number + 3) >> 2, four, (zero,) * 6)
        to = (t >> 3) * ROWS + (t & 7) * 6
        for i in range(6):
            out_ref[pl.ds(to + i, 6, stride=TILES), :] = acc[i]
        return carry

    lax.fori_loop(0, 32, target, 0)


def reduce_kernel(in_ref, out_ref, got_ref, pack_ref, halo_ref, send_sem, recv_sem):
    clus, direction, core, x, z = position()
    after = (clus, lax.rem(direction + 1, N_DIR))
    before = (clus, lax.rem(direction + N_DIR - 1, N_DIR))
    me = (1 - core) * z + core * x
    others = [lax.rem(me + r, 4) for r in (1, 2, 3)]
    peers = [(reduce_member(core, x, z, k), direction) for k in others]
    enter([after, before, *peers])
    copies = []
    for r, (k, peer) in enumerate(zip(others, peers)):
        copy = pltpu.make_async_remote_copy(
            in_ref.at[pl.ds(pl.multiple_of(k * ROWS, 8), ROWS)], got_ref.at[r],
            send_sem.at[2 + r], recv_sem.at[2 + r], device_id=peer, device_id_type=MESH,
        )
        copy.start()
        copies.append(copy)
    for copy in copies:
        copy.wait_recv()
    out_ref[TILES : TILES + ROWS, :] = (in_ref[pl.ds(pl.multiple_of(me * ROWS, 8), ROWS), :] + got_ref[0]) + (
        got_ref[1] + got_ref[2]
    )
    pack_ref[0] = jnp.where(even_lanes(), out_ref[2 * TILES : 3 * TILES, :], out_ref[TILES : 2 * TILES, :])
    pack_ref[1] = out_ref[6 * TILES : 7 * TILES, :]
    backward = pltpu.make_async_remote_copy(
        pack_ref.at[0], halo_ref.at[0], send_sem.at[0], recv_sem.at[0], device_id=before, device_id_type=MESH
    )
    forward = pltpu.make_async_remote_copy(
        pack_ref.at[1], halo_ref.at[1], send_sem.at[1], recv_sem.at[1], device_id=after, device_id_type=MESH
    )
    backward.start()
    forward.start()
    backward.wait_recv()
    forward.wait_recv()
    out_ref[7 * TILES : 8 * TILES, :] = halo_ref[0]
    out_ref[0:TILES, :] = halo_ref[1]
    for copy in (backward, forward, *copies):
        copy.wait_send()


def disaggregate_kernel(
    parent_ref, octant_ref, inc_ref, right_ref, left_ref, phases_ref,
    out_ref, r_ref, base_ref, table_ref, tile_ref, sem,
):
    copy = pltpu.make_async_copy(phases_ref.at[lax.axis_index("dir")], base_ref, sem)
    copy.start()
    for t in range(TILES):
        tile_ref[8 * t : 8 * t + 8, :] = inc_ref[pl.ds(t, 8, stride=TILES), :]
    copy.wait()
    octant_tables(base_ref, table_ref)

    def child(k, carry):
        g, o = parent_ref[0, k], octant_ref[k]
        for c in range(3):
            re = tile_ref[pl.ds(pl.multiple_of((g * 6 + c) * 8, 8), 8), :]
            im = tile_ref[pl.ds(pl.multiple_of((g * 6 + 3 + c) * 8, 8), 8), :]
            fr = table_ref[pl.ds(pl.multiple_of((o * 6 + c) * 8, 8), 8), :]
            fi = table_ref[pl.ds(pl.multiple_of((o * 6 + 3 + c) * 8, 8), 8), :]
            r_ref[pl.ds(pl.multiple_of(k * 16, 8), 8), 128 * c : 128 * c + 128] = re * fr + im * fi
            r_ref[pl.ds(pl.multiple_of(k * 16 + 8, 8), 8), 128 * c : 128 * c + 128] = im * fr - re * fi
        return carry

    lax.fori_loop(0, KIDS, child, 0, unroll=4)
    for n in range(6):
        hi, lo = split(r_ref[128 * n : 128 * n + 128, :])
        e = dot3((hi[:, :256], lo[:, :256]), (right_ref[0, 0], right_ref[1, 0]))
        o = dot3((hi[:, 128:], lo[:, 128:]), (right_ref[0, 1], right_ref[1, 1]))
        v = split(jnp.concatenate([e, o], axis=0))
        out_ref[8 * n : 8 * n + 8] = dot3((left_ref[0], left_ref[1]), v).reshape(8, 2, 8, 128)


VMEM_SPEC = pl.BlockSpec(memory_space=pltpu.VMEM)
SMEM_SPEC = pl.BlockSpec(memory_space=pltpu.SMEM)
ANY_SPEC = pl.BlockSpec(memory_space=pl.ANY)
LIMIT = 48 * 2**20


def f32(*shape):
    return jax.ShapeDtypeStruct(shape, jnp.float32)


def on_device(child, table, child_parent, child_octant, partner_src, partner_off, partner_count):
    up_left, up_right, down_right, down_left, phases = (jnp.asarray(a) for a in constants())
    flat_table = table.reshape(OFFSETS, 2, 18, 128).transpose(0, 2, 1, 3).reshape(OFFSETS * 36, 128)
    vm = functools.partial(pltpu.VMEM, dtype=jnp.float32)
    part, lists = pl.pallas_call(
        aggregate_kernel,
        out_shape=(f32(8 * TILES, 128), jax.ShapeDtypeStruct((32, 128), jnp.int32)),
        in_specs=[SMEM_SPEC] * 2 + [VMEM_SPEC] * 6 + [ANY_SPEC],
        out_specs=(VMEM_SPEC, VMEM_SPEC),
        scratch_shapes=[
            vm((768, 384)), vm((144, 128)), vm((384, 128)), vm((384, 128)), pltpu.VMEM((32, 128), jnp.int32),
            pltpu.SemaphoreType.DMA,
        ],
        compiler_params=pltpu.CompilerParams(vmem_limit_bytes=LIMIT),
        name="aggregate",
    )(child_parent, child_octant, child, partner_src, partner_off, partner_count.reshape(1, 128), up_left, up_right, phases)
    sources = pl.pallas_call(
        gather_kernel,
        out_shape=f32(4 * ROWS, 128),
        in_specs=[VMEM_SPEC],
        out_specs=VMEM_SPEC,
        scratch_shapes=[vm((2, TILES, 128)), pltpu.SemaphoreType.DMA((5,)), pltpu.SemaphoreType.DMA((5,))],
        compiler_params=pltpu.CompilerParams(collective_id=0, has_side_effects=True, vmem_limit_bytes=LIMIT),
        name="gather",
    )(part)
    partial = pl.pallas_call(
        translate_kernel,
        out_shape=f32(4 * ROWS, 128),
        in_specs=[SMEM_SPEC, VMEM_SPEC, VMEM_SPEC],
        out_specs=VMEM_SPEC,
        scratch_shapes=[vm((OFFSETS * 36 + 40, 128))],
        compiler_params=pltpu.CompilerParams(vmem_limit_bytes=LIMIT),
        name="translate",
    )(lists, flat_table, sources)
    incoming = pl.pallas_call(
        reduce_kernel,
        out_shape=f32(8 * TILES, 128),
        in_specs=[VMEM_SPEC],
        out_specs=VMEM_SPEC,
        scratch_shapes=[
            vm((3, ROWS, 128)), vm((2, TILES, 128)), vm((2, TILES, 128)),
            pltpu.SemaphoreType.DMA((5,)), pltpu.SemaphoreType.DMA((5,)),
        ],
        compiler_params=pltpu.CompilerParams(collective_id=1, has_side_effects=True, vmem_limit_bytes=LIMIT),
        name="reduce",
    )(partial)
    return pl.pallas_call(
        disaggregate_kernel,
        out_shape=f32(KIDS, 2, 8, 128),
        in_specs=[SMEM_SPEC] * 2 + [VMEM_SPEC] * 3 + [ANY_SPEC],
        out_specs=VMEM_SPEC,
        scratch_shapes=[
            vm((768, 384)), vm((144, 128)), vm((384, 128)), vm((384, 128)), pltpu.SemaphoreType.DMA,
        ],
        compiler_params=pltpu.CompilerParams(vmem_limit_bytes=LIMIT),
        name="disaggregate",
    )(child_parent, child_octant, incoming, down_right, down_left, phases)


def solution(mesh):
    return jax.shard_map(
        on_device,
        mesh=mesh,
        in_specs=(P("clus", None, "dir", None), P(None, None, "dir"), P("clus", None), P("clus"), P(), P(), P()),
        out_specs=P("clus", None, "dir", None),
        check_vma=False,
    )
```

time: 205 us -> 71 us (0.35)
  waiting for transfers between devices: 68.7 us -> 0 us
  Pallas kernels: 0 us -> 53.8 us
  other arithmetic: 37.1 us -> 0 us
  starting transfers between devices: 30.9 us -> 0 us
  local copies, waits for them, and re-layouts: 46 us -> 16.5 us
  between operations: 13.6 us -> 0.15 us
  matrix products: 7.91 us -> 0 us
    pallas_call x0 -> x5, Pallas kernels: none -> 53.8 us  [the longest x1 23.2 us: on_device(): pl.pallas_call(gather_kernel, out_shape=f32(4 * ROWS, 128), in_specs=[VME...]
    all_gather x1 -> x0, waiting for transfers between devices: 53.1 us -> none  [on_device(): sources = lax.all_gather(flattened, 'clus', axis=0, tiled=True)]
    gather x2 -> x0, local copies, waits for them, and re-layouts: 43.1 us -> none  [the longest x1 22.7 us: translate(): picked = sources[partner_src]]
    ppermute x4 -> x0, starting transfers between devices: 30.9 us -> none  [the longest x2 27 us: with_halo(): before = lax.ppermute(last, axis, up)]
    reduce_sum x1 -> x0, other arithmetic: 22.2 us -> none  [translate(): jnp.sum(operator[:, :, 0] * picked[:, :, 0] - operator[:, :, 1] * picked[...]
    ppermute x4 -> x0, waiting for transfers between devices: 15.6 us -> none  [the longest x2 15.5 us: with_halo(): after = lax.ppermute(initial, axis, down)]
    unnamed x10 -> x29, local copies, waits for them, and re-layouts: 0.03 us -> 8.53 us
    mul x5 -> x0, other arithmetic: 8.5 us -> none  [the longest x1 8.36 us: translate(): table[partner_off].astype(jnp.float32) * live_mask[:, :, None, None]]
  transfers between devices with their start and end apart: 5 -> 0, of which waited for: 4 -> 0; matrix products, arithmetic and copies ran while one was open for 15% -> 0% of each run, Pallas kernels for 0% -> 0%
where the time goes in v1:
time: 71 us; the launch traced here: 70.4 us
  Pallas kernels  53.8 us (76%)
  local copies, waits for them, and re-layouts  16.5 us (23%)
    pallas_call x1, Pallas kernels, on_device(): pl.pallas_call(gather_kernel, out_shape=f32(4 * ROWS, 128), in_specs=[VME...  23.2 us
    pallas_call x1, Pallas kernels, on_device(): pl.pallas_call(reduce_kernel, out_shape=f32(8 * TILES, 128), in_specs=[VM...  17.4 us
    unnamed x29, local copies, waits for them, and re-layouts  8.53 us
    pallas_call x1, Pallas kernels, on_device(): pl.pallas_call(translate_kernel, out_shape=f32(4 * ROWS, 128), in_specs=[...  6.02 us
    transpose x1, local copies, waits for them, and re-layouts, on_device(): table.reshape(OFFSETS, 2, 18, 128).transpose(0, 2, 1, 3)  5.09 us
    pallas_call x1, Pallas kernels, on_device(): pl.pallas_call(disaggregate_kernel, out_shape=f32(KIDS, 2, 8, 128), in_sp...  3.77 us
    pallas_call x1, Pallas kernels, on_device(): pl.pallas_call(aggregate_kernel, out_shape=(f32(8 * TILES, 128), jax.Shap...  3.39 us
    reshape x1, local copies, waits for them, and re-layouts, on_device(): table.reshape(OFFSETS, 2, 18, 128).transpose(0, 2, 1, 3)  2.87 us

profile of v1, /device:TPU:1, one launch (start us, length us, event | category | flops | bytes accessed | tf_op | source)
XLA Modules:
  0.0 70.4 jit_solution(7322061481524122769)
XLA Ops:
  0.0 0.8 %copy.16.src_ref = s32[128,56]{1,0:T(8,128)S(1)} copy(s32[128,56]{0,1:T(8,128)} %param.16) | data formatting | bytes 57344 | tf_op args[4]
  0.8 0.8 %copy.17.off_ref = s32[128,56]{1,0:T(8,128)S(1)} copy(s32[128,56]{0,1:T(8,128)} %param.17) | data formatting | bytes 57344 | tf_op args[5]
  1.7 0.0 copy-start
  1.7 1.7 %copy-done = f32[32,144,128]{2,1,0:T(8,128)S(1)} copy-done((f32[32,144,128]{2,1,0:T(8,128)S(1)}, f32[32,144,128]{2,1,0:T(8,128)}, u32[]{:S(2)}) %copy-start) | copy-done | bytes 2359320
  3.4 1.0 %copy-done.2 = f32[48,2,8,128]{3,2,1,0:T(8,128)S(1)} copy-done((f32[48,2,8,128]{3,2,1,0:T(8,128)S(1)}, f32[48,2,8,128]{3,2,1,0:T(8,128)}, u32[]{:S(2)}) %copy-start.2) | copy-done | bytes 393240
  4.4 1.0 %copy-done.3 = bf16[2,256,384]{2,1,0:T(8,128)(2,1)S(1)} copy-done((bf16[2,256,384]{2,1,0:T(8,128)(2,1)S(1)}, bf16[2,256,384]{2,1,0:T(8,128)(2,1)}, u32[]{:S(2)}) %copy-start.3) | copy-done | bytes 393240
  5.4 0.9 %copy-done.6 = bf16[2,256,128]{2,1,0:T(8,128)(2,1)S(1)} copy-done((bf16[2,256,128]{2,1,0:T(8,128)(2,1)S(1)}, bf16[2,256,128]{2,1,0:T(8,128)(2,1)}, u32[]{:S(2)}) %copy-start.6) | copy-done | bytes 131096
  6.3 0.7 copy-done.7
  6.9 0.7 copy-done.9
  7.6 0.7 copy-done.11
  8.2 3.4 %aggregate.1 = (f32[384,128]{1,0:T(8,128)S(1)}, s32[32,128]{1,0:T(8,128)S(1)}) custom-call(s32[1,48]{1,0:T(1,128)S(1)} %copy-done.7, s32[48]{0:T(128)S(1)} %copy-done.9, f32[48,2,8,128]{3,2,1,0:T(8,128)S(1)} %copy-done.2, s32[128,56]{1,0:T(8,128)S(1)} %copy.16.src_ref, s32[128,56]{1,0:T(8,128)S(1)} %copy.17.off_ref, s32[1,128]{1,0:T(1,128)S(1)} %bitcast.6, ...), custom_call_target="tpu_custom_call" | custom-call | tf_op jit(solution)/shard_map/aggregate/pallas_call | solution.py:400
  11.6 0.0 copy-done.12
  11.6 0.3 copy.18
  11.9 2.9 %reshape.10 = bf16[316,2,18,128]{3,2,0,1:T(8,128)(2,1)} reshape(bf16[316,2,2304]{2,0,1:T(8,128)(2,1)S(1)} %copy.18) | data formatting | bytes 5824512 | tf_op jit(solution)/shard_map/reshape | solution.py:398
  14.8 5.1 %copy.19 = bf16[316,18,2,128]{3,2,1,0:T(2,128)(2,1)S(1)} copy(bf16[316,18,2,128]{3,1,0,2:T(8,128)(2,1)} %bitcast.7) | data formatting | bytes 5824512 | tf_op jit(solution)/shard_map/transpose | solution.py:398
  19.9 0.0 copy-start.1
  19.9 0.0 copy-start.4
  19.9 0.0 copy-start.5
  19.9 0.0 copy-start.8
  20.0 0.0 copy-start.10
  20.0 23.2 %gather.1.s_ref = f32[1152,128]{1,0:T(8,128)S(1)} custom-call(f32[384,128]{1,0:T(8,128)S(1)} %get-tuple-element.8.part_ref), custom_call_target="tpu_custom_call" | custom-call | tf_op jit(solution)/shard_map/gather/pallas_call | solution.py:412
  43.2 6.0 %translate.1.in_ref = f32[1152,128]{1,0:T(8,128)S(1)} custom-call(s32[32,128]{1,0:T(8,128)S(1)} %get-tuple-element.7.list_ref, bf16[11376,128]{1,0:T(8,128)(2,1)S(1)} %bitcast.5, f32[1152,128]{1,0:T(8,128)S(1)} %gather.1.s_ref), custom_call_target="tpu_custom_call" | custom-call | tf_op jit(solution)/shard_map/translate/pallas_call | solution.py:421
  49.2 17.4 %reduce.1.inc_ref = f32[384,128]{1,0:T(8,128)S(1)} custom-call(f32[1152,128]{1,0:T(8,128)S(1)} %translate.1.in_ref), custom_call_target="tpu_custom_call" | custom-call | tf_op jit(solution)/shard_map/reduce/pallas_call | solution.py:430
  66.7 3.8 %disaggregate.1 = f32[48,2,8,128]{3,2,1,0:T(8,128)} custom-call(s32[1,48]{1,0:T(1,128)S(1)} %copy-done.8, s32[48]{0:T(128)S(1)} %copy-done.10, f32[384,128]{1,0:T(8,128)S(1)} %reduce.1.inc_ref, bf16[2,2,256,128]{3,2,1,0:T(8,128)(2,1)S(1)} %copy-done.4, bf16[2,128,256]{2,1,0:T(8,128)(2,1)S(1)} %copy-done.5, f32[32,144,128]{2,1,0:T(8,128)S(1)} %copy-done.1), custom_call_target="tpu_custom_call" | custom-call | tf_op jit(solution)/shard_map/disaggregate/pallas_call | solution.py:442
  (12 shorter events, 0.0 us)
Async XLA Ops:
  1.7 1.7 %copy-start = (f32[32,144,128]{2,1,0:T(8,128)S(1)}, f32[32,144,128]{2,1,0:T(8,128)}, u32[]{:S(2)}) copy-start(f32[32,144,128]{2,1,0:T(8,128)} %constant.14.clone.phases_ref) | copy-start | bytes 7077892
  3.4 1.0 %copy-start.2 = (f32[48,2,8,128]{3,2,1,0:T(8,128)S(1)}, f32[48,2,8,128]{3,2,1,0:T(8,128)}, u32[]{:S(2)}) copy-start(f32[48,2,8,128]{3,2,1,0:T(8,128)} %child_ref.1) | copy-start | bytes 1179652
  4.4 1.0 %copy-start.3 = (bf16[2,256,384]{2,1,0:T(8,128)(2,1)S(1)}, bf16[2,256,384]{2,1,0:T(8,128)(2,1)}, u32[]{:S(2)}) copy-start(bf16[2,256,384]{2,1,0:T(8,128)(2,1)} %constant.11.clone.right_ref) | copy-start | bytes 1179652
  5.4 0.9 %copy-start.6 = (bf16[2,256,128]{2,1,0:T(8,128)(2,1)S(1)}, bf16[2,256,128]{2,1,0:T(8,128)(2,1)}, u32[]{:S(2)}) copy-start(bf16[2,256,128]{2,1,0:T(8,128)(2,1)} %constant.10.clone.left_ref) | copy-start | bytes 393220
  6.3 0.7 copy-start.7
  6.9 0.7 copy-start.9
  7.6 0.7 copy-start.11
  8.2 3.4 %copy-start.12 = (bf16[316,2,2304]{2,1,0:T(2,128)(2,1)S(1)}, bf16[316,2,2304]{2,1,0:T(2,128)(2,1)}, u32[]{:S(2)}) copy-start(bf16[316,2,2304]{2,1,0:T(2,128)(2,1)} %param.13) | copy-start | bytes 8736772
  19.9 46.7 %copy-start.1 = (f32[32,144,128]{2,1,0:T(8,128)S(1)}, f32[32,144,128]{2,1,0:T(8,128)}, u32[]{:S(2)}) copy-start(f32[32,144,128]{2,1,0:T(8,128)} %constant.14.clone.phases_ref) | copy-start | bytes 7077892
  19.9 46.7 %copy-start.4 = (bf16[2,2,256,128]{3,2,1,0:T(8,128)(2,1)S(1)}, bf16[2,2,256,128]{3,2,1,0:T(8,128)(2,1)}, u32[]{:S(2)}) copy-start(bf16[2,2,256,128]{3,2,1,0:T(8,128)(2,1)} %constant.12.clone.right_ref) | copy-start | bytes 786436
  19.9 46.7 %copy-start.5 = (bf16[2,128,256]{2,1,0:T(8,128)(2,1)S(1)}, bf16[2,128,256]{2,1,0:T(8,128)(2,1)}, u32[]{:S(2)}) copy-start(bf16[2,128,256]{2,1,0:T(8,128)(2,1)} %constant.13.clone.left_ref) | copy-start | bytes 393220
  19.9 46.7 %copy-start.8 = (s32[1,48]{1,0:T(1,128)S(1)}, s32[1,48]{1,0:T(1,128)}, u32[]{:S(2)}) copy-start(s32[1,48]{1,0:T(1,128)} %parent_ref.3) | copy-start | bytes 580
  20.0 46.7 %copy-start.10 = (s32[48]{0:T(128)S(1)}, s32[48]{0:T(128)}, u32[]{:S(2)}) copy-start(s32[48]{0:T(128)} %octant_ref.3) | copy-start | bytes 580

commit v2 on v1

v2 whole, which is shorter than its diff:
```python
import functools
import math

import jax
import jax.numpy as jnp
import ml_dtypes
import numpy as np
from jax import lax
from jax.experimental import pallas as pl
from jax.experimental.pallas import tpu as pltpu
from jax.sharding import PartitionSpec as P

NT_C, NP_C, NT_P, NP_P = 128, 256, 192, 384
OFFSETS = 316
N_CLUS, N_DIR = 16, 32
PAR, KIDS = 8, 48
TILES = PAR * 6
MESH = pl.DeviceIdType.MESH
EVEN = np.array([-2, 0, 2, 4, 6, 8, 10, 14])
ODD = np.array([-1, 1, 3, 5, 7, 9, 11, 13])


def lagrange(t):
    out = []
    for m in range(5):
        w = np.ones_like(t)
        for n in range(5):
            if n != m:
                w = w * (t - n) / (m - n)
        out.append(w)
    return out


def polar_matrix():
    x = (np.arange(NT_P) + 0.5) * NT_C / NT_P - 0.5
    s = np.clip(np.floor(x + 0.5).astype(int) - 2, 0, NT_C - 5)
    w = lagrange(x - s)
    m = np.zeros((NT_P, NT_C))
    for k in range(5):
        m[np.arange(NT_P), s + k] = w[k]
    return m


def azimuth_rows(rows):
    x = rows * NP_C / NP_P
    b = np.floor(x + 0.5).astype(int)
    w = lagrange(x - b + 2)
    m = np.zeros((len(rows), 8))
    for k in range(5):
        for j in range(len(rows)):
            i = b[j] + k - 2
            if 0 <= i < 8:
                m[j, i] = w[k][j]
    return m


def halves(a):
    a = a.astype(np.float32)
    hi = a.astype(ml_dtypes.bfloat16)
    lo = (a - hi.astype(np.float32)).astype(ml_dtypes.bfloat16)
    return np.stack([hi, lo])


def in_tiles(even, odd):
    return np.stack([even[:, :128], np.concatenate([even[:, 128:], odd[:, :64]], 1), odd[:, 64:]])


@functools.cache
def constants():
    p = polar_matrix()
    ae, ao = azimuth_rows(EVEN), azimuth_rows(ODD)
    eye = np.eye(16)
    up_left = halves(np.concatenate([np.kron(eye, ae), np.kron(eye, ao)], 0))
    w = np.zeros((256, 384))
    w[:128, :192] = p.T
    w[128:, 192:] = p.T
    up_right = halves(w)
    down_right = halves(np.stack([w[:128, :256].T, w[128:, 128:].T]))
    down_left = halves(np.concatenate([np.kron(eye, ae.T), np.kron(eye, ao.T)], 1))
    theta = math.pi * (np.arange(NT_P) + 0.5) / NT_P
    phases = np.zeros((N_DIR, 3, 2, 3, 8, 128))
    for d in range(N_DIR):
        angle = []
        for rows in (EVEN, ODD):
            phi = 2 * math.pi * ((12 * d + rows) % NP_P) / NP_P
            angle.append(
                8 * math.pi
                * np.stack(
                    [
                        np.sin(theta) * np.cos(phi)[:, None],
                        np.sin(theta) * np.sin(phi)[:, None],
                        np.cos(theta) * np.ones((8, 1)),
                    ]
                )
            )
        for k in range(3):
            t = in_tiles(angle[0][k], angle[1][k])
            phases[d, k] = np.stack([np.cos(t), np.sin(t)])
    return up_left, up_right, down_right, down_left, phases.reshape(N_DIR, 144, 128).astype(np.float32)


def split(x):
    hi = x.astype(jnp.bfloat16)
    return hi, (x - hi.astype(jnp.float32)).astype(jnp.bfloat16)


def dot3(a, b):
    f = functools.partial(jnp.dot, preferred_element_type=jnp.float32)
    return f(a[0], b[0]) + (f(a[1], b[0]) + f(a[0], b[1]))


def position():
    clus, direction = lax.axis_index("clus"), lax.axis_index("dir")
    core = lax.rem(direction, 2)
    x, z = lax.rem(clus, 4), lax.div(clus, 4)
    return clus, direction, core, x, z


def gather_member(core, x, z, k):
    return (1 - core) * (z * 4 + k) + core * (k * 4 + x)


def reduce_member(core, x, z, k):
    return (1 - core) * (k * 4 + x) + core * (z * 4 + k)


def octant_tables(base, table):
    def tile(k, a, c):
        r = (k * 6 + a * 3 + c) * 8
        return base[r : r + 8, :]

    for c in range(3):
        ar, ai, br, bi, cr, ci = (tile(k, a, c) for k in range(3) for a in range(2))
        rr, ii, ri, ir = ar * br, ai * bi, ar * bi, ai * br
        for sx, sy, re, im in ((1, 1, rr - ii, ri + ir), (1, -1, rr + ii, ir - ri)):
            pr, pi, qr, qi = re * cr, im * ci, re * ci, im * cr
            for sz, fr, fi in ((1, pr - pi, qr + qi), (-1, pr + pi, qi - qr)):
                for sign in (1, -1):
                    o = (sx * sign < 0) + 2 * (sy * sign < 0) + 4 * (sz * sign < 0)
                    table[o * 6 + c] = fr
                    table[o * 6 + 3 + c] = fi if sign > 0 else -fi


def aligned(i, n=8):
    return pl.multiple_of(i, n)


def build_index(parent_ref, src_ref, off_ref, count_ref, key_ref):
    clus, direction, core, x, z = position()
    src = src_ref[...]
    off = off_ref[...]
    slot = lax.broadcasted_iota(jnp.int32, src.shape, 0)
    own_x, own_z = (src >> 3) & 3, src >> 5
    here = jnp.where(core == 0, own_z, own_x) == jnp.where(core == 0, z, x)
    local = jnp.where(core == 0, own_x, own_z) * 8 + (src & 7)
    local = jnp.where(here & (slot < count_ref[...]), local, -1)
    which = lax.broadcasted_iota(jnp.int32, (32, 128), 0)
    key = jnp.full((32, 128), OFFSETS, jnp.int32)
    for p in range(src.shape[0]):
        key = jnp.where(which == local[p : p + 1], off[p : p + 1], key)
    key_ref[0:32, :] = key
    parent = lax.broadcasted_iota(jnp.int32, (8, KIDS), 0)
    start = jnp.sum((parent_ref[...] < parent).astype(jnp.int32), axis=1, keepdims=True)
    number = jnp.sum((parent_ref[...] == parent).astype(jnp.int32), axis=1, keepdims=True)
    lane = lax.broadcasted_iota(jnp.int32, (8, 128), 1)
    own = jnp.where(lane < number, start + lane, KIDS)
    key_ref[32:40, :] = jnp.where(lane < 8, own, jnp.minimum(start + lane - 8, KIDS - 1))


def even_lanes():
    column = lax.rem(lax.broadcasted_iota(jnp.int32, (TILES, 128), 0), 3)
    lane = lax.broadcasted_iota(jnp.int32, (TILES, 128), 1)
    return (column == 0) | ((column == 1) & (lane < 64))


PAIRS = ((2, 3, 4), (0, 1, 5))
PIECES = (((768, 0, 1152),), ((0, 0, 768), (1920, 768, 384)))
HALF = 1152


def relay(tile_ref, s_ref, part, first):
    def parent(g, carry):
        for n, q in enumerate(PAIRS[part]):
            for c in range(3):
                lanes = slice(128 * (3 * n + c), 128 * (3 * n + c) + 128)
                s_ref[first + g, :, lanes] = tile_ref[pl.ds((g * 6 + c) * 8 + q + 1, 2, stride=24), :]
        return carry

    lax.fori_loop(0, PAR, parent, 0)


def unrelay(sum_ref, tile_ref, part):
    def parent(g, carry):
        for n, q in enumerate(PAIRS[part]):
            for c in range(3):
                lanes = slice(128 * (3 * n + c), 128 * (3 * n + c) + 128)
                tile_ref[pl.ds((g * 6 + c) * 8 + q + 1, 2, stride=24), :] = sum_ref[g, :, lanes]
        return carry

    lax.fori_loop(0, PAR, parent, 0)


def swap(s_ref, x_ref, block):
    def source(i, carry):
        at = block * 8 + i
        x_ref[at, 0:1, :] = s_ref[at, 1:2, :]
        x_ref[at, 1:2, :] = s_ref[at, 0:1, :]
        return carry

    lax.fori_loop(0, PAR, source, 0, unroll=2)


GROUP = 4


def add_pairs(part, key_ref, table_ref, s_ref, x_ref, block, first_target, acc):
    acc = [list(a) for a in acc]
    pieces = PIECES[part]
    for u in range(PAR):
        source = block * 8 + u
        for p, (at, to, n) in enumerate(pieces):
            s = s_ref[source, :, to : to + n]
            x = x_ref[source, :, to : to + n]
            for j in range(GROUP):
                t = table_ref[key_ref[source, first_target + j], :, at : at + n].astype(jnp.float32)
                acc[j][p] = acc[j][p] + t * s
                acc[j][len(pieces) + p] = acc[j][len(pieces) + p] + t * x
    return tuple(tuple(a) for a in acc)


def middle_kernel(
    parent_hbm, octant_hbm, child_hbm, src_hbm, off_hbm, count_hbm, table_hbm, left_hbm, right_hbm, phases_hbm,
    out_ref,
    parent_ref, octant_ref, child_ref, src_ref, off_ref, count_ref, table_ref, left_ref, right_ref, base_ref,
    key_ref, index_ref, z_ref, phase_ref, tile_ref, pack_ref, halo_ref,
    sa_ref, sb_ref, xa_ref, xb_ref, acca_ref, accb_ref, pa_ref, pb_ref, gota_ref, gotb_ref, sum_ref,
    local_sem, send_sem, recv_sem,
):
    clus, direction, core, x, z = position()
    after = (clus, lax.rem(direction + 1, N_DIR))
    before = (clus, lax.rem(direction + N_DIR - 1, N_DIR))
    source_me = (1 - core) * x + core * z
    target_me = (1 - core) * z + core * x
    source_blocks = [lax.rem(source_me + r, 4) for r in range(4)]
    target_blocks = [lax.rem(target_me + r, 4) for r in range(4)]
    source_peers = [(gather_member(core, x, z, k), direction) for k in source_blocks[1:]]
    target_peers = [(reduce_member(core, x, z, k), direction) for k in target_blocks[1:]]
    barrier = pltpu.get_barrier_semaphore()
    peers = [after, before, *source_peers, *target_peers]
    for peer in peers:
        pl.semaphore_signal(barrier, inc=1, device_id=peer, device_id_type=MESH)

    def fetch(n, src, dst):
        copy = pltpu.make_async_copy(src, dst, local_sem.at[n])
        copy.start()
        return copy

    small = [
        fetch(0, parent_hbm, parent_ref),
        fetch(1, src_hbm, src_ref),
        fetch(2, off_hbm, off_ref),
        fetch(3, count_hbm, count_ref),
    ]
    kids = [
        fetch(4 + n, child_hbm.at[pl.ds(16 * n, 16)], child_ref.at[pl.ds(16 * n, 16)]) for n in range(3)
    ]
    weights = [fetch(7, left_hbm, left_ref), fetch(8, right_hbm, right_ref)]
    base = fetch(9, phases_hbm.at[direction], base_ref)
    octants = fetch(10, octant_hbm, octant_ref)
    z_ref[2 * KIDS : 2 * KIDS + 2] = jnp.zeros((2, 8, 384), jnp.float32)
    table = fetch(11, table_hbm, table_ref.at[pl.ds(0, OFFSETS)])
    table_ref[OFFSETS] = jnp.zeros((2, 2304), jnp.bfloat16)

    for copy in small:
        copy.wait()
    build_index(parent_ref, src_ref, off_ref, count_ref, key_ref)
    index = fetch(0, key_ref, index_ref)
    for copy in weights:
        copy.wait()
    for n in range(6):
        if n % 2 == 0:
            kids[n // 2].wait()
        xs = split(child_ref[8 * n : 8 * n + 8].reshape(128, 128))
        eo = dot3((left_ref[0], left_ref[1]), xs)
        y = split(jnp.concatenate([eo[:128], eo[128:]], axis=1))
        z_ref[16 * n : 16 * n + 16] = dot3(y, (right_ref[0], right_ref[1])).reshape(16, 8, 384)
    base.wait()
    octant_tables(base_ref, phase_ref)
    octants.wait()
    index.wait()

    def parent(g, carry):
        acc = [jnp.zeros((8, 128), jnp.float32) for _ in range(6)]
        for m in range(8):
            k = index_ref[32 + g, m]
            o = octant_ref[index_ref[32 + g, 8 + m]]
            for c in range(3):
                re = z_ref[k * 2, :, 128 * c : 128 * c + 128]
                im = z_ref[k * 2 + 1, :, 128 * c : 128 * c + 128]
                fr = phase_ref[o * 6 + c]
                fi = phase_ref[o * 6 + 3 + c]
                acc[c] = acc[c] + (re * fr - im * fi)
                acc[3 + c] = acc[3 + c] + (re * fi + im * fr)
        for t in range(6):
            tile_ref[pl.ds(aligned((g * 6 + t) * 8), 8), :] = acc[t]
        return carry

    lax.fori_loop(0, PAR, parent, 0)

    pl.semaphore_wait(barrier, len(peers))

    def send(n, src, dst, peer):
        copy = pltpu.make_async_remote_copy(
            src, dst, send_sem.at[n], recv_sem.at[n], device_id=peer, device_id_type=MESH
        )
        copy.start()
        return copy

    pack_ref[0] = tile_ref[pl.ds(7, TILES, stride=8), :]
    forward = send(0, pack_ref.at[0], halo_ref.at[0], after)
    pack_ref[1] = tile_ref[pl.ds(0, TILES, stride=8), :]
    backward = send(1, pack_ref.at[1], halo_ref.at[1], before)
    own = source_me * 8
    relay(tile_ref, sa_ref, 0, own)
    block_a = sa_ref.at[pl.ds(own, 8)]
    gather_a = [send(2 + r, block_a, block_a, peer) for r, peer in enumerate(source_peers)]
    swap(sa_ref, xa_ref, source_me)
    table.wait()

    parts = ((sa_ref, xa_ref, acca_ref, pa_ref), (sb_ref, xb_ref, accb_ref, pb_ref))

    def own_pass(part):
        s_ref, x_ref, acc_ref, _ = parts[part]
        k = len(PIECES[part])

        def group(i, carry):
            j, g = lax.div(i, 2), lax.rem(i, 2) * GROUP
            zero = tuple(jnp.zeros((2, n), jnp.float32) for _ in range(2) for _, _, n in PIECES[part])
            acc = add_pairs(
                part, index_ref, table_ref, s_ref, x_ref, source_me, reduce_member(core, x, z, j) * 8 + g, (zero,) * GROUP
            )
            for t in range(GROUP):
                for p, (_, to, n) in enumerate(PIECES[part]):
                    acc_ref[j * 8 + g + t, 0, :, to : to + n] = acc[t][p]
                    acc_ref[j * 8 + g + t, 1, :, to : to + n] = acc[t][k + p]
            return carry

        lax.fori_loop(0, 32 // GROUP, group, 0)

    def rest_pass(part, j):
        s_ref, x_ref, acc_ref, p_ref = parts[part]
        k = len(PIECES[part])

        def group(i, carry):
            g = i * GROUP
            acc = tuple(
                tuple(acc_ref[j * 8 + g + t, h, :, to : to + n] for h in range(2) for _, to, n in PIECES[part])
                for t in range(GROUP)
            )

            def block(r, acc):
                return add_pairs(
                    part, index_ref, table_ref, s_ref, x_ref, lax.rem(source_me + r, 4),
                    reduce_member(core, x, z, j) * 8 + g, acc,
                )

            acc = lax.fori_loop(1, 4, block, acc)
            for t in range(GROUP):
                for p, (_, to, n) in enumerate(PIECES[part]):
                    a, b = acc[t][p], acc[t][k + p]
                    p_ref[j * 8 + g + t, 0:1, to : to + n] = a[0:1] - a[1:2]
                    p_ref[j * 8 + g + t, 1:2, to : to + n] = b[0:1] + b[1:2]
            return carry

        lax.fori_loop(0, PAR // GROUP, group, 0)

    own_pass(0)

    even = even_lanes()
    forward.wait_recv()
    got = halo_ref[0]
    at1, at2, at6 = (pl.ds(s, TILES, stride=8) for s in (1, 2, 6))
    tile_ref[at1, :] = tile_ref[at1, :] + jnp.where(even, 0.0, got)
    tile_ref[at2, :] = tile_ref[at2, :] + jnp.where(even, got, 0.0)
    backward.wait_recv()
    tile_ref[at6, :] = tile_ref[at6, :] + halo_ref[1]
    relay(tile_ref, sb_ref, 1, own)
    block_b = sb_ref.at[pl.ds(own, 8)]
    gather_b = [send(5 + r, block_b, block_b, peer) for r, peer in enumerate(source_peers)]
    swap(sb_ref, xb_ref, source_me)
    own_pass(1)

    reduces = []
    for part, gathers, got_ref in ((0, gather_a, gota_ref), (1, gather_b, gotb_ref)):
        s_ref, x_ref, _, p_ref = parts[part]
        for r, copy in enumerate(gathers):
            copy.wait_recv()
        for r in range(1, 4):
            swap(s_ref, x_ref, source_blocks[r])
        for r in range(1, 4):
            rest_pass(part, target_blocks[r])
            reduces.append(
                send(8 + 3 * part + r - 1, p_ref.at[pl.ds(target_blocks[r] * 8, 8)], got_ref.at[r - 1], target_peers[r - 1])
            )
        rest_pass(part, target_blocks[0])

    def total(part, got_ref):
        p_ref = parts[part][3]
        for copy in reduces[3 * part : 3 * part + 3]:
            copy.wait_recv()

        def parent(g, carry):
            sum_ref[g] = (p_ref[target_me * 8 + g] + got_ref[0, g]) + (got_ref[1, g] + got_ref[2, g])
            return carry

        lax.fori_loop(0, PAR, parent, 0)
        unrelay(sum_ref, out_ref, part)

    total(0, gota_ref)
    total(1, gotb_ref)
    pack_ref[2] = jnp.where(even, out_ref[at2, :], out_ref[at1, :])
    last_back = send(14, pack_ref.at[2], halo_ref.at[2], before)
    pack_ref[3] = out_ref[at6, :]
    last_on = send(15, pack_ref.at[3], halo_ref.at[3], after)
    for copy in (forward, backward, *gather_a, *gather_b, *reduces):
        copy.wait_send()
    last_back.wait()
    last_on.wait()
    out_ref[pl.ds(7, TILES, stride=8), :] = halo_ref[2]
    out_ref[pl.ds(0, TILES, stride=8), :] = halo_ref[3]


def disaggregate_kernel(
    parent_ref, octant_ref, tile_ref, right_ref, left_ref, phases_ref,
    out_ref, r_ref, base_ref, table_ref, sem,
):
    copy = pltpu.make_async_copy(phases_ref.at[lax.axis_index("dir")], base_ref, sem)
    copy.start()
    copy.wait()
    octant_tables(base_ref, table_ref)

    def child(k, carry):
        g, o = parent_ref[0, k], octant_ref[k]
        for c in range(3):
            re = tile_ref[pl.ds(pl.multiple_of((g * 6 + c) * 8, 8), 8), :]
            im = tile_ref[pl.ds(pl.multiple_of((g * 6 + 3 + c) * 8, 8), 8), :]
            fr = table_ref[o * 6 + c]
            fi = table_ref[o * 6 + 3 + c]
            r_ref[pl.ds(pl.multiple_of(k * 16, 8), 8), 128 * c : 128 * c + 128] = re * fr + im * fi
            r_ref[pl.ds(pl.multiple_of(k * 16 + 8, 8), 8), 128 * c : 128 * c + 128] = im * fr - re * fi
        return carry

    lax.fori_loop(0, KIDS, child, 0, unroll=4)
    for n in range(6):
        hi, lo = split(r_ref[128 * n : 128 * n + 128, :])
        e = dot3((hi[:, :256], lo[:, :256]), (right_ref[0, 0], right_ref[1, 0]))
        o = dot3((hi[:, 128:], lo[:, 128:]), (right_ref[0, 1], right_ref[1, 1]))
        v = split(jnp.concatenate([e, o], axis=0))
        out_ref[8 * n : 8 * n + 8] = dot3((left_ref[0], left_ref[1]), v).reshape(8, 2, 8, 128)


VMEM_SPEC = pl.BlockSpec(memory_space=pltpu.VMEM)
SMEM_SPEC = pl.BlockSpec(memory_space=pltpu.SMEM)
ANY_SPEC = pl.BlockSpec(memory_space=pl.ANY)
HBM_SPEC = pl.BlockSpec(memory_space=pltpu.HBM)
LIMIT = 63 * 2**20


def f32(*shape):
    return jax.ShapeDtypeStruct(shape, jnp.float32)


def on_device(child, table, child_parent, child_octant, partner_src, partner_off, partner_count):
    up_left, up_right, down_right, down_left, phases = (jnp.asarray(a) for a in constants())
    vm = functools.partial(pltpu.VMEM, dtype=jnp.float32)
    ints = functools.partial(pltpu.VMEM, dtype=jnp.int32)
    bf16 = functools.partial(pltpu.VMEM, dtype=jnp.bfloat16)
    incoming = pl.pallas_call(
        middle_kernel,
        out_shape=f32(8 * TILES, 128),
        in_specs=[HBM_SPEC] * 10,
        out_specs=VMEM_SPEC,
        scratch_shapes=[
            ints((1, KIDS)), pltpu.SMEM((KIDS,), jnp.int32), vm((KIDS, 2, 8, 128)), ints((56, 128)), ints((56, 128)),
            ints((1, 128)), bf16((OFFSETS + 1, 2, 2304)), bf16((2, 256, 128)), bf16((2, 256, 384)), vm((144, 128)),
            ints((40, 128)), pltpu.SMEM((40, 128), jnp.int32), vm((2 * KIDS + 2, 8, 384)), vm((48, 8, 128)), vm((384, 128)),
            vm((4, TILES, 128)), vm((4, TILES, 128)),
            *[vm((32, 2, HALF))] * 4, *[vm((32, 2, 2, HALF))] * 2, *[vm((32, 2, HALF))] * 2,
            *[vm((3, 8, 2, HALF))] * 2, vm((8, 2, HALF)),
            pltpu.SemaphoreType.DMA((12,)), pltpu.SemaphoreType.DMA((16,)), pltpu.SemaphoreType.DMA((16,)),
        ],
        compiler_params=pltpu.CompilerParams(collective_id=0, has_side_effects=True, vmem_limit_bytes=LIMIT),
        name="middle",
    )(
        child_parent, child_octant, child, partner_src.T, partner_off.T, partner_count.reshape(1, 128), table,
        up_left, up_right, phases,
    )
    return pl.pallas_call(
        disaggregate_kernel,
        out_shape=f32(KIDS, 2, 8, 128),
        in_specs=[SMEM_SPEC] * 2 + [VMEM_SPEC] * 3 + [ANY_SPEC],
        out_specs=VMEM_SPEC,
        scratch_shapes=[vm((768, 384)), vm((144, 128)), vm((48, 8, 128)), pltpu.SemaphoreType.DMA],
        compiler_params=pltpu.CompilerParams(vmem_limit_bytes=LIMIT),
        name="disaggregate",
    )(child_parent, child_octant, incoming, down_right, down_left, phases)


def solution(mesh):
    return jax.shard_map(
        on_device,
        mesh=mesh,
        in_specs=(P("clus", None, "dir", None), P(None, None, "dir"), P("clus", None), P("clus"), P(), P(), P()),
        out_specs=P("clus", None, "dir", None),
        check_vma=False,
    )
```

time: 71 us -> 43 us (0.61)
  local copies, waits for them, and re-layouts: 16.5 us -> 0 us
  Pallas kernels: 53.8 us -> 42.2 us
    pallas_call x4 -> x1, Pallas kernels: 50 us -> 37.1 us  [on_device(): pl.pallas_call(middle_kernel, out_shape=f32(8 * TILES, 128), in_specs=[HB...]
    unnamed x29 -> x0, local copies, waits for them, and re-layouts: 8.53 us -> none
    transpose x1 -> x0, local copies, waits for them, and re-layouts: 5.09 us -> none  [on_device(): table.reshape(OFFSETS, 2, 18, 128).transpose(0, 2, 1, 3)]
    reshape x1 -> x0, local copies, waits for them, and re-layouts: 2.87 us -> none  [on_device(): table.reshape(OFFSETS, 2, 18, 128).transpose(0, 2, 1, 3)]
    pallas_call x1, Pallas kernels: 3.77 us -> 5.03 us  [on_device(): pl.pallas_call(disaggregate_kernel, out_shape=f32(KIDS, 2, 8, 128), in_sp...]
where the time goes in v2:
time: 43 us; the launch traced here: 42.2 us
  Pallas kernels  42.2 us (98%)
    pallas_call x1, Pallas kernels, on_device(): pl.pallas_call(middle_kernel, out_shape=f32(8 * TILES, 128), in_specs=[HB...  37.1 us
    pallas_call x1, Pallas kernels, on_device(): pl.pallas_call(disaggregate_kernel, out_shape=f32(KIDS, 2, 8, 128), in_sp...  5.03 us

profile of v2, /device:TPU:1, one launch (start us, length us, event | category | flops | bytes accessed | tf_op | source)
XLA Modules:
  0.0 42.2 jit_solution(1412110835200843121)
XLA Ops:
  0.0 37.1 %middle.1.tile_ref = f32[384,128]{1,0:T(8,128)} custom-call(s32[1,48]{1,0:T(1,128)} %parent_ref.1, s32[48]{0:T(128)} %octant_ref.1, f32[48,2,8,128]{3,2,1,0:T(8,128)} %child_hbm.1, s32[56,128]{1,0:T(8,128)} %bitcast.3, s32[56,128]{1,0:T(8,128)} %bitcast.4, s32[1,128]{1,0:T(1,128)} %bitcast.5, bf16[316,2,2304]{2,1,0:T(2,128)(2,1)} %table_hbm.1, ...), custom_call_target="tpu_custom_call" | custom-call | tf_op jit(solution)/shard_map/middle/pallas_call | solution.py:478
  37.1 5.0 %disaggregate.1 = f32[48,2,8,128]{3,2,1,0:T(8,128)} custom-call(s32[1,48]{1,0:T(1,128)} %parent_ref.1, s32[48]{0:T(128)} %octant_ref.1, f32[384,128]{1,0:T(8,128)} %middle.1.tile_ref, bf16[2,2,256,128]{3,2,1,0:T(8,128)(2,1)} %constant.12.clone.right_ref, bf16[2,128,256]{2,1,0:T(8,128)(2,1)} %constant.13.clone.left_ref, ...), custom_call_target="tpu_custom_call" | custom-call | tf_op jit(solution)/shard_map/disaggregate/pallas_call | solution.py:498

commit v3 on v2

--- a/solution.py
+++ b/solution.py
@@ -124,7 +124,7 @@
     return (1 - core) * (k * 4 + x) + core * (z * 4 + k)
 
 
-def octant_tables(base, table):
+def octant_tables(base, table, edge):
     def tile(k, a, c):
         r = (k * 6 + a * 3 + c) * 8
         return base[r : r + 8, :]
@@ -137,15 +137,26 @@
             for sz, fr, fi in ((1, pr - pi, qr + qi), (-1, pr + pi, qi - qr)):
                 for sign in (1, -1):
                     o = (sx * sign < 0) + 2 * (sy * sign < 0) + 4 * (sz * sign < 0)
-                    table[o * 6 + c] = fr
-                    table[o * 6 + 3 + c] = fi if sign > 0 else -fi
+                    for t, f in ((c, fr), (3 + c, fi if sign > 0 else -fi)):
+                        table[o * 6 + t] = f
+                        edge[0, t, o : o + 1, :] = f[0:1]
+                        edge[1, t, o : o + 1, :] = f[7:8]
 
 
 def aligned(i, n=8):
     return pl.multiple_of(i, n)
 
 
-def build_index(parent_ref, src_ref, off_ref, count_ref, key_ref):
+def build_kids(parent_ref, kids_ref):
+    parent = lax.broadcasted_iota(jnp.int32, (8, KIDS), 0)
+    start = jnp.sum((parent_ref[...] < parent).astype(jnp.int32), axis=1, keepdims=True)
+    number = jnp.sum((parent_ref[...] == parent).astype(jnp.int32), axis=1, keepdims=True)
+    lane = lax.broadcasted_iota(jnp.int32, (8, 128), 1)
+    own = jnp.where(lane < number, start + lane, KIDS)
+    kids_ref[...] = jnp.where(lane < 8, own, jnp.minimum(start + lane - 8, KIDS - 1))
+
+
+def build_index(src_ref, off_ref, count_ref, key_ref):
     clus, direction, core, x, z = position()
     src = src_ref[...]
     off = off_ref[...]
@@ -158,13 +169,21 @@
     key = jnp.full((32, 128), OFFSETS, jnp.int32)
     for p in range(src.shape[0]):
         key = jnp.where(which == local[p : p + 1], off[p : p + 1], key)
-    key_ref[0:32, :] = key
-    parent = lax.broadcasted_iota(jnp.int32, (8, KIDS), 0)
-    start = jnp.sum((parent_ref[...] < parent).astype(jnp.int32), axis=1, keepdims=True)
-    number = jnp.sum((parent_ref[...] == parent).astype(jnp.int32), axis=1, keepdims=True)
-    lane = lax.broadcasted_iota(jnp.int32, (8, 128), 1)
-    own = jnp.where(lane < number, start + lane, KIDS)
-    key_ref[32:40, :] = jnp.where(lane < 8, own, jnp.minimum(start + lane - 8, KIDS - 1))
+    key_ref[...] = key
+
+
+def one_hot(row, n):
+    square = (KIDS, KIDS)
+    diagonal = lax.broadcasted_iota(jnp.int32, square, 0) == lax.broadcasted_iota(jnp.int32, square, 1)
+    column = jnp.sum(jnp.where(diagonal, row, 0), axis=1, keepdims=True)
+    hot = column == lax.broadcasted_iota(jnp.int32, (KIDS, n), 1)
+    return jnp.where(hot, 1.0, 0.0).astype(jnp.bfloat16)
+
+
+def pick(hot, tiles):
+    hi, lo = split(jnp.concatenate(tiles, axis=1))
+    f = functools.partial(jnp.dot, preferred_element_type=jnp.float32)
+    return f(hot, hi) + f(hot, lo)
 
 
 def even_lanes():
@@ -230,9 +249,11 @@
 
 def middle_kernel(
     parent_hbm, octant_hbm, child_hbm, src_hbm, off_hbm, count_hbm, table_hbm, left_hbm, right_hbm, phases_hbm,
+    right2_hbm, left2_hbm,
     out_ref,
-    parent_ref, octant_ref, child_ref, src_ref, off_ref, count_ref, table_ref, left_ref, right_ref, base_ref,
-    key_ref, index_ref, z_ref, phase_ref, tile_ref, pack_ref, halo_ref,
+    parent_ref, octants_ref, parents_ref, octant_ref, child_ref, src_ref, off_ref, count_ref, table_ref, left_ref,
+    right_ref, base_ref, right2_ref, left2_ref, edge_ref,
+    key_ref, index_ref, kids_ref, kid_ref, z_ref, phase_ref, tile_ref, inc_ref, r_ref, pack_ref, halo_ref,
     sa_ref, sb_ref, xa_ref, xb_ref, acca_ref, accb_ref, pa_ref, pb_ref, gota_ref, gotb_ref, sum_ref,
     local_sem, send_sem, recv_sem,
 ):
@@ -241,8 +262,9 @@
     before = (clus, lax.rem(direction + N_DIR - 1, N_DIR))
     source_me = (1 - core) * x + core * z
     target_me = (1 - core) * z + core * x
-    source_blocks = [lax.rem(source_me + r, 4) for r in range(4)]
-    target_blocks = [lax.rem(target_me + r, 4) for r in range(4)]
+    source_blocks, target_blocks = (
+        [me, 3 - me, lax.rem(me + 2, 4), me + 1 - 2 * lax.rem(me, 2)] for me in (source_me, target_me)
+    )
     source_peers = [(gather_member(core, x, z, k), direction) for k in source_blocks[1:]]
     target_peers = [(reduce_member(core, x, z, k), direction) for k in target_blocks[1:]]
     barrier = pltpu.get_barrier_semaphore()
@@ -255,45 +277,50 @@
         copy.start()
         return copy
 
-    small = [
-        fetch(0, parent_hbm, parent_ref),
-        fetch(1, src_hbm, src_ref),
-        fetch(2, off_hbm, off_ref),
-        fetch(3, count_hbm, count_ref),
+    parents = fetch(0, parent_hbm, parent_ref)
+    first = [
+        fetch(1, left_hbm, left_ref),
+        fetch(2, child_hbm, child_ref),
+        fetch(3, right_hbm, right_ref),
+        fetch(4, phases_hbm.at[direction], base_ref),
+        fetch(5, src_hbm, src_ref),
+        fetch(6, off_hbm, off_ref),
+        fetch(7, count_hbm, count_ref),
     ]
-    kids = [
-        fetch(4 + n, child_hbm.at[pl.ds(16 * n, 16)], child_ref.at[pl.ds(16 * n, 16)]) for n in range(3)
+    second = [
+        fetch(8, octant_hbm, octant_ref),
+        fetch(9, parent_hbm, parents_ref),
+        fetch(10, octant_hbm, octants_ref),
     ]
-    weights = [fetch(7, left_hbm, left_ref), fetch(8, right_hbm, right_ref)]
-    base = fetch(9, phases_hbm.at[direction], base_ref)
-    octants = fetch(10, octant_hbm, octant_ref)
     z_ref[2 * KIDS : 2 * KIDS + 2] = jnp.zeros((2, 8, 384), jnp.float32)
-    table = fetch(11, table_hbm, table_ref.at[pl.ds(0, OFFSETS)])
     table_ref[OFFSETS] = jnp.zeros((2, 2304), jnp.bfloat16)
-
-    for copy in small:
+    parents.wait()
+    build_kids(parent_ref, kids_ref)
+    kids = fetch(0, kids_ref, kid_ref)
+    for copy in first:
         copy.wait()
-    build_index(parent_ref, src_ref, off_ref, count_ref, key_ref)
-    index = fetch(0, key_ref, index_ref)
-    for copy in weights:
-        copy.wait()
+    third = [
+        fetch(11, table_hbm, table_ref.at[pl.ds(0, OFFSETS)]),
+        fetch(12, right2_hbm, right2_ref),
+        fetch(13, left2_hbm, left2_ref),
+    ]
+    build_index(src_ref, off_ref, count_ref, key_ref)
     for n in range(6):
-        if n % 2 == 0:
-            kids[n // 2].wait()
         xs = split(child_ref[8 * n : 8 * n + 8].reshape(128, 128))
         eo = dot3((left_ref[0], left_ref[1]), xs)
         y = split(jnp.concatenate([eo[:128], eo[128:]], axis=1))
         z_ref[16 * n : 16 * n + 16] = dot3(y, (right_ref[0], right_ref[1])).reshape(16, 8, 384)
-    base.wait()
-    octant_tables(base_ref, phase_ref)
-    octants.wait()
-    index.wait()
+    octant_tables(base_ref, phase_ref, edge_ref)
+    index = fetch(1, key_ref, index_ref)
+    kids.wait()
+    for copy in second:
+        copy.wait()
 
     def parent(g, carry):
         acc = [jnp.zeros((8, 128), jnp.float32) for _ in range(6)]
         for m in range(8):
-            k = index_ref[32 + g, m]
-            o = octant_ref[index_ref[32 + g, 8 + m]]
+            k = kid_ref[g, m]
+            o = octant_ref[0, kid_ref[g, 8 + m]]
             for c in range(3):
                 re = z_ref[k * 2, :, 128 * c : 128 * c + 128]
                 im = z_ref[k * 2 + 1, :, 128 * c : 128 * c + 128]
@@ -325,7 +352,8 @@
     block_a = sa_ref.at[pl.ds(own, 8)]
     gather_a = [send(2 + r, block_a, block_a, peer) for r, peer in enumerate(source_peers)]
     swap(sa_ref, xa_ref, source_me)
-    table.wait()
+    for copy in (index, *third):
+        copy.wait()
 
     parts = ((sa_ref, xa_ref, acca_ref, pa_ref), (sb_ref, xb_ref, accb_ref, pb_ref))
 
@@ -414,54 +442,66 @@
             return carry
 
         lax.fori_loop(0, PAR, parent, 0)
-        unrelay(sum_ref, out_ref, part)
-
+        unrelay(sum_ref, tile_ref, part)
+
+    total(1, gotb_ref)
+    pack_ref[2] = jnp.where(even, tile_ref[at2, :], tile_ref[at1, :])
+    last_back = send(14, pack_ref.at[2], halo_ref.at[2], before)
+    pack_ref[3] = tile_ref[at6, :]
+    last_on = send(15, pack_ref.at[3], halo_ref.at[3], after)
     total(0, gota_ref)
-    total(1, gotb_ref)
-    pack_ref[2] = jnp.where(even, out_ref[at2, :], out_ref[at1, :])
-    last_back = send(14, pack_ref.at[2], halo_ref.at[2], before)
-    pack_ref[3] = out_ref[at6, :]
-    last_on = send(15, pack_ref.at[3], halo_ref.at[3], after)
+    pair = lax.broadcasted_iota(jnp.int32, (8, 128), 0)
+    inside = (pair > 0) & (pair < 7)
+    for t in range(TILES):
+        inc_ref[t] = jnp.where(inside, tile_ref[8 * t : 8 * t + 8, :], 0.0)
+
+    def child(k, carry):
+        g, o = parents_ref[0, k], octant_ref[0, k]
+        for c in range(3):
+            re, im = inc_ref[g * 6 + c], inc_ref[g * 6 + 3 + c]
+            fr, fi = phase_ref[o * 6 + c], phase_ref[o * 6 + 3 + c]
+            r_ref[k * 2, :, 128 * c : 128 * c + 128] = re * fr + im * fi
+            r_ref[k * 2 + 1, :, 128 * c : 128 * c + 128] = im * fr - re * fi
+        return carry
+
+    lax.fori_loop(0, KIDS, child, 0, unroll=4)
+
+    def to_child(r):
+        hi, lo = split(r)
+        return (
+            dot3((hi[:, :256], lo[:, :256]), (right2_ref[0, 0], right2_ref[1, 0])),
+            dot3((hi[:, 128:], lo[:, 128:]), (right2_ref[0, 1], right2_ref[1, 1])),
+        )
+
+    for n in range(6):
+        v = split(jnp.concatenate(to_child(r_ref[16 * n : 16 * n + 16].reshape(128, 384)), axis=0))
+        out_ref[128 * n : 128 * n + 128, :] = dot3((left2_ref[0], left2_ref[1]), v)
+    hot_parent, hot_octant = one_hot(parent_ref[...], 8), one_hot(octants_ref[...], 8)
+    shifts = [pick(hot_octant, [edge_ref[e, t] for t in range(6)]) for e in range(2)]
     for copy in (forward, backward, *gather_a, *gather_b, *reduces):
         copy.wait_send()
     last_back.wait()
     last_on.wait()
-    out_ref[pl.ds(7, TILES, stride=8), :] = halo_ref[2]
-    out_ref[pl.ds(0, TILES, stride=8), :] = halo_ref[3]
-
-
-def disaggregate_kernel(
-    parent_ref, octant_ref, tile_ref, right_ref, left_ref, phases_ref,
-    out_ref, r_ref, base_ref, table_ref, sem,
-):
-    copy = pltpu.make_async_copy(phases_ref.at[lax.axis_index("dir")], base_ref, sem)
-    copy.start()
-    copy.wait()
-    octant_tables(base_ref, table_ref)
-
-    def child(k, carry):
-        g, o = parent_ref[0, k], octant_ref[k]
-        for c in range(3):
-            re = tile_ref[pl.ds(pl.multiple_of((g * 6 + c) * 8, 8), 8), :]
-            im = tile_ref[pl.ds(pl.multiple_of((g * 6 + 3 + c) * 8, 8), 8), :]
-            fr = table_ref[o * 6 + c]
-            fi = table_ref[o * 6 + 3 + c]
-            r_ref[pl.ds(pl.multiple_of(k * 16, 8), 8), 128 * c : 128 * c + 128] = re * fr + im * fi
-            r_ref[pl.ds(pl.multiple_of(k * 16 + 8, 8), 8), 128 * c : 128 * c + 128] = im * fr - re * fi
-        return carry
-
-    lax.fori_loop(0, KIDS, child, 0, unroll=4)
-    for n in range(6):
-        hi, lo = split(r_ref[128 * n : 128 * n + 128, :])
-        e = dot3((hi[:, :256], lo[:, :256]), (right_ref[0, 0], right_ref[1, 0]))
-        o = dot3((hi[:, 128:], lo[:, 128:]), (right_ref[0, 1], right_ref[1, 1]))
-        v = split(jnp.concatenate([e, o], axis=0))
-        out_ref[8 * n : 8 * n + 8] = dot3((left_ref[0], left_ref[1]), v).reshape(8, 2, 8, 128)
+    rows = []
+    for e in range(2):
+        values = pick(hot_parent, [halo_ref[3 - e, pl.ds(t, 8, stride=6), :] for t in range(6)])
+        re, im, fr, fi = values[:, :384], values[:, 384:], shifts[e][:, :384], shifts[e][:, 384:]
+        rows += [re * fr + im * fi, im * fr - re * fi]
+    even_part, odd_part = to_child(jnp.concatenate(rows, axis=0))
+    weight_even, weight_odd = azimuth_rows(EVEN), azimuth_rows(ODD)
+    for e, s in enumerate((0, 7)):
+        for a in range(2):
+            at = (2 * e + a) * KIDS
+            for i in range(8):
+                we, wo = float(weight_even[s, i]), float(weight_odd[s, i])
+                if we or wo:
+                    place = pl.ds(a * 8 + i, KIDS, stride=16)
+                    out_ref[place, :] = out_ref[place, :] + (
+                        we * even_part[at : at + KIDS] + wo * odd_part[at : at + KIDS]
+                    )
 
 
 VMEM_SPEC = pl.BlockSpec(memory_space=pltpu.VMEM)
-SMEM_SPEC = pl.BlockSpec(memory_space=pltpu.SMEM)
-ANY_SPEC = pl.BlockSpec(memory_space=pl.ANY)
 HBM_SPEC = pl.BlockSpec(memory_space=pltpu.HBM)
 LIMIT = 63 * 2**20
 
@@ -475,35 +515,30 @@
     vm = functools.partial(pltpu.VMEM, dtype=jnp.float32)
     ints = functools.partial(pltpu.VMEM, dtype=jnp.int32)
     bf16 = functools.partial(pltpu.VMEM, dtype=jnp.bfloat16)
-    incoming = pl.pallas_call(
+    scalars = functools.partial(pltpu.SMEM, dtype=jnp.int32)
+    out = pl.pallas_call(
         middle_kernel,
-        out_shape=f32(8 * TILES, 128),
-        in_specs=[HBM_SPEC] * 10,
+        out_shape=f32(KIDS * 16, 128),
+        in_specs=[HBM_SPEC] * 12,
         out_specs=VMEM_SPEC,
         scratch_shapes=[
-            ints((1, KIDS)), pltpu.SMEM((KIDS,), jnp.int32), vm((KIDS, 2, 8, 128)), ints((56, 128)), ints((56, 128)),
-            ints((1, 128)), bf16((OFFSETS + 1, 2, 2304)), bf16((2, 256, 128)), bf16((2, 256, 384)), vm((144, 128)),
-            ints((40, 128)), pltpu.SMEM((40, 128), jnp.int32), vm((2 * KIDS + 2, 8, 384)), vm((48, 8, 128)), vm((384, 128)),
-            vm((4, TILES, 128)), vm((4, TILES, 128)),
+            ints((1, KIDS)), ints((1, KIDS)), scalars((1, KIDS)), scalars((1, KIDS)), vm((KIDS, 2, 8, 128)),
+            ints((56, 128)), ints((56, 128)), ints((1, 128)), bf16((OFFSETS + 1, 2, 2304)), bf16((2, 256, 128)),
+            bf16((2, 256, 384)), vm((144, 128)), bf16((2, 2, 256, 128)), bf16((2, 128, 256)), vm((2, 6, 8, 128)),
+            ints((32, 128)), scalars((32, 128)), ints((8, 128)), scalars((8, 128)),
+            vm((2 * KIDS + 2, 8, 384)), vm((48, 8, 128)), vm((8 * TILES, 128)), vm((TILES, 8, 128)),
+            vm((2 * KIDS, 8, 384)), vm((4, TILES, 128)), vm((4, TILES, 128)),
             *[vm((32, 2, HALF))] * 4, *[vm((32, 2, 2, HALF))] * 2, *[vm((32, 2, HALF))] * 2,
             *[vm((3, 8, 2, HALF))] * 2, vm((8, 2, HALF)),
-            pltpu.SemaphoreType.DMA((12,)), pltpu.SemaphoreType.DMA((16,)), pltpu.SemaphoreType.DMA((16,)),
+            pltpu.SemaphoreType.DMA((14,)), pltpu.SemaphoreType.DMA((16,)), pltpu.SemaphoreType.DMA((16,)),
         ],
         compiler_params=pltpu.CompilerParams(collective_id=0, has_side_effects=True, vmem_limit_bytes=LIMIT),
         name="middle",
     )(
-        child_parent, child_octant, child, partner_src.T, partner_off.T, partner_count.reshape(1, 128), table,
-        up_left, up_right, phases,
+        child_parent, child_octant.reshape(1, KIDS), child, partner_src.T, partner_off.T, partner_count.reshape(1, 128),
+        table, up_left, up_right, phases, down_right, down_left,
     )
-    return pl.pallas_call(
-        disaggregate_kernel,
-        out_shape=f32(KIDS, 2, 8, 128),
-        in_specs=[SMEM_SPEC] * 2 + [VMEM_SPEC] * 3 + [ANY_SPEC],
-        out_specs=VMEM_SPEC,
-        scratch_shapes=[vm((768, 384)), vm((144, 128)), vm((48, 8, 128)), pltpu.SemaphoreType.DMA],
-        compiler_params=pltpu.CompilerParams(vmem_limit_bytes=LIMIT),
-        name="disaggregate",
-    )(child_parent, child_octant, incoming, down_right, down_left, phases)
+    return out.reshape(KIDS, 2, 8, 128)
 
 
 def solution(mesh):

time: 43 us -> 42.6 us (level)
  the two profiles are of different devices: /device:TPU:1 before, /device:TPU:2 now
where the time goes in v3:
time: 42.6 us; the launch traced here: 42.4 us
  Pallas kernels  40.6 us (95%)
  local copies, waits for them, and re-layouts  1.77 us (4%)
    pallas_call x1, Pallas kernels, on_device(): pl.pallas_call(middle_kernel, out_shape=f32(KIDS * 16, 128), in_specs=[HB...  40.6 us
    unnamed x1, local copies, waits for them, and re-layouts  1.77 us

profile of v3, /device:TPU:2, one launch (start us, length us, event | category | flops | bytes accessed | tf_op | source)
XLA Modules:
  0.0 42.4 jit_solution(11129404798380745340)
XLA Ops:
  0.0 40.6 %middle.1 = f32[768,128]{1,0:T(8,128)} custom-call(s32[1,48]{1,0:T(1,128)} %parent_hbm.1, s32[1,48]{1,0:T(1,128)} %bitcast.8, f32[48,2,8,128]{3,2,1,0:T(8,128)} %child_hbm.1, s32[56,128]{1,0:T(8,128)} %bitcast.6, s32[56,128]{1,0:T(8,128)} %bitcast.7, s32[1,128]{1,0:T(1,128)} %bitcast.9, bf16[316,2,2304]{2,1,0:T(2,128)(2,1)} %table_hbm.1, ...), custom_call_target="tpu_custom_call" | custom-call | tf_op jit(solution)/shard_map/middle/pallas_call | solution.py:519
  40.6 1.8 %copy.14 = f32[48,2,8,128]{3,2,1,0:T(8,128)} copy(f32[48,2,8,128]{3,2,1,0:T(8,128)} %bitcast.5) | data formatting | bytes 786432

commit v4 on v3

--- a/solution.py
+++ b/solution.py
@@ -253,7 +253,7 @@
     out_ref,
     parent_ref, octants_ref, parents_ref, octant_ref, child_ref, src_ref, off_ref, count_ref, table_ref, left_ref,
     right_ref, base_ref, right2_ref, left2_ref, edge_ref,
-    key_ref, index_ref, kids_ref, kid_ref, z_ref, phase_ref, tile_ref, inc_ref, r_ref, pack_ref, halo_ref,
+    key_ref, index_ref, kids_ref, kid_ref, y_ref, z_ref, phase_ref, tile_ref, inc_ref, r_ref, pack_ref, halo_ref,
     sa_ref, sb_ref, xa_ref, xb_ref, acca_ref, accb_ref, pa_ref, pb_ref, gota_ref, gotb_ref, sum_ref,
     local_sem, send_sem, recv_sem,
 ):
@@ -309,7 +309,9 @@
         xs = split(child_ref[8 * n : 8 * n + 8].reshape(128, 128))
         eo = dot3((left_ref[0], left_ref[1]), xs)
         y = split(jnp.concatenate([eo[:128], eo[128:]], axis=1))
-        z_ref[16 * n : 16 * n + 16] = dot3(y, (right_ref[0], right_ref[1])).reshape(16, 8, 384)
+        for h in range(2):
+            y_ref[h, 128 * n : 128 * n + 128, :] = y[h]
+    z_ref[0 : 2 * KIDS] = dot3((y_ref[0], y_ref[1]), (right_ref[0], right_ref[1])).reshape(2 * KIDS, 8, 384)
     octant_tables(base_ref, phase_ref, edge_ref)
     index = fetch(1, key_ref, index_ref)
     kids.wait()
@@ -418,19 +420,26 @@
     swap(sb_ref, xb_ref, source_me)
     own_pass(1)
 
-    reduces = []
-    for part, gathers, got_ref in ((0, gather_a, gota_ref), (1, gather_b, gotb_ref)):
-        s_ref, x_ref, _, p_ref = parts[part]
-        for r, copy in enumerate(gathers):
+    def gathered(part, gathers):
+        for copy in gathers:
             copy.wait_recv()
         for r in range(1, 4):
-            swap(s_ref, x_ref, source_blocks[r])
-        for r in range(1, 4):
-            rest_pass(part, target_blocks[r])
-            reduces.append(
-                send(8 + 3 * part + r - 1, p_ref.at[pl.ds(target_blocks[r] * 8, 8)], got_ref.at[r - 1], target_peers[r - 1])
-            )
-        rest_pass(part, target_blocks[0])
+            swap(parts[part][0], parts[part][1], source_blocks[r])
+
+    def reduce_to(part, r, got_ref):
+        block = parts[part][3].at[pl.ds(target_blocks[r] * 8, 8)]
+        return send(8 + 3 * part + r - 1, block, got_ref.at[r - 1], target_peers[r - 1])
+
+    gathered(0, gather_a)
+    for r in range(4):
+        rest_pass(0, target_blocks[r])
+    gathered(1, gather_b)
+    reduces_b = []
+    for r in range(1, 4):
+        rest_pass(1, target_blocks[r])
+        reduces_b.append(reduce_to(1, r, gotb_ref))
+    reduces = [reduce_to(0, r, gota_ref) for r in range(1, 4)] + reduces_b
+    rest_pass(1, target_blocks[0])
 
     def total(part, got_ref):
         p_ref = parts[part][3]
@@ -526,7 +535,7 @@
             ints((56, 128)), ints((56, 128)), ints((1, 128)), bf16((OFFSETS + 1, 2, 2304)), bf16((2, 256, 128)),
             bf16((2, 256, 384)), vm((144, 128)), bf16((2, 2, 256, 128)), bf16((2, 128, 256)), vm((2, 6, 8, 128)),
             ints((32, 128)), scalars((32, 128)), ints((8, 128)), scalars((8, 128)),
-            vm((2 * KIDS + 2, 8, 384)), vm((48, 8, 128)), vm((8 * TILES, 128)), vm((TILES, 8, 128)),
+            bf16((2, 768, 256)), vm((2 * KIDS + 2, 8, 384)), vm((48, 8, 128)), vm((8 * TILES, 128)), vm((TILES, 8, 128)),
             vm((2 * KIDS, 8, 384)), vm((4, TILES, 128)), vm((4, TILES, 128)),
             *[vm((32, 2, HALF))] * 4, *[vm((32, 2, 2, HALF))] * 2, *[vm((32, 2, HALF))] * 2,
             *[vm((3, 8, 2, HALF))] * 2, vm((8, 2, HALF)),

time: 42.6 us -> 39 us (0.915)
  the two profiles are of different devices: /device:TPU:2 before, /device:TPU:1 now
where the time goes in v4:
time: 39 us; the launch traced here: 38.6 us
  Pallas kernels  36.8 us (94%)
  local copies, waits for them, and re-layouts  1.77 us (5%)
    pallas_call x1, Pallas kernels, on_device(): pl.pallas_call(middle_kernel, out_shape=f32(KIDS * 16, 128), in_specs=[HB...  36.8 us
    unnamed x1, local copies, waits for them, and re-layouts  1.77 us

profile of v4, /device:TPU:1, one launch (start us, length us, event | category | flops | bytes accessed | tf_op | source)
XLA Modules:
  0.0 38.6 jit_solution(8028629917491530454)
XLA Ops:
  0.0 36.8 %middle.1 = f32[768,128]{1,0:T(8,128)} custom-call(s32[1,48]{1,0:T(1,128)} %parent_hbm.1, s32[1,48]{1,0:T(1,128)} %bitcast.8, f32[48,2,8,128]{3,2,1,0:T(8,128)} %child_hbm.1, s32[56,128]{1,0:T(8,128)} %bitcast.6, s32[56,128]{1,0:T(8,128)} %bitcast.7, s32[1,128]{1,0:T(1,128)} %bitcast.9, bf16[316,2,2304]{2,1,0:T(2,128)(2,1)} %table_hbm.1, ...), custom_call_target="tpu_custom_call" | custom-call | tf_op jit(solution)/shard_map/middle/pallas_call | solution.py:528
  36.8 1.8 %copy.14 = f32[48,2,8,128]{3,2,1,0:T(8,128)} copy(f32[48,2,8,128]{3,2,1,0:T(8,128)} %bitcast.5) | data formatting | bytes 786432

commit v5 on v4

--- a/solution.py
+++ b/solution.py
@@ -41,6 +41,9 @@
     return m
 
 
+SCALE = 243
+
+
 def azimuth_rows(rows):
     x = rows * NP_C / NP_P
     b = np.floor(x + 0.5).astype(int)
@@ -50,8 +53,8 @@
         for j in range(len(rows)):
             i = b[j] + k - 2
             if 0 <= i < 8:
-                m[j, i] = w[k][j]
-    return m
+                m[j, i] = w[k][j] * SCALE
+    return np.round(m)
 
 
 def halves(a):
@@ -70,13 +73,14 @@
     p = polar_matrix()
     ae, ao = azimuth_rows(EVEN), azimuth_rows(ODD)
     eye = np.eye(16)
-    up_left = halves(np.concatenate([np.kron(eye, ae), np.kron(eye, ao)], 0))
+    up_left = np.concatenate([np.kron(eye, ae), np.kron(eye, ao)], 0).astype(ml_dtypes.bfloat16)
     w = np.zeros((256, 384))
     w[:128, :192] = p.T
     w[128:, 192:] = p.T
+    w = w / SCALE
     up_right = halves(w)
     down_right = halves(np.stack([w[:128, :256].T, w[128:, 128:].T]))
-    down_left = halves(np.concatenate([np.kron(eye, ae.T), np.kron(eye, ao.T)], 1))
+    down_left = np.concatenate([np.kron(eye, ae.T), np.kron(eye, ao.T)], 1).astype(ml_dtypes.bfloat16)
     theta = math.pi * (np.arange(NT_P) + 0.5) / NT_P
     phases = np.zeros((N_DIR, 3, 2, 3, 8, 128))
     for d in range(N_DIR):
@@ -109,6 +113,11 @@
     return f(a[0], b[0]) + (f(a[1], b[0]) + f(a[0], b[1]))
 
 
+def dot2(a, b):
+    f = functools.partial(jnp.dot, preferred_element_type=jnp.float32)
+    return f(a, b[0]) + f(a, b[1])
+
+
 def position():
     clus, direction = lax.axis_index("clus"), lax.axis_index("dir")
     core = lax.rem(direction, 2)
@@ -181,9 +190,7 @@
 
 
 def pick(hot, tiles):
-    hi, lo = split(jnp.concatenate(tiles, axis=1))
-    f = functools.partial(jnp.dot, preferred_element_type=jnp.float32)
-    return f(hot, hi) + f(hot, lo)
+    return dot2(hot, split(jnp.concatenate(tiles, axis=1)))
 
 
 def even_lanes():
@@ -307,7 +314,7 @@
     build_index(src_ref, off_ref, count_ref, key_ref)
     for n in range(6):
         xs = split(child_ref[8 * n : 8 * n + 8].reshape(128, 128))
-        eo = dot3((left_ref[0], left_ref[1]), xs)
+        eo = dot2(left_ref[...], xs)
         y = split(jnp.concatenate([eo[:128], eo[128:]], axis=1))
         for h in range(2):
             y_ref[h, 128 * n : 128 * n + 128, :] = y[h]
@@ -377,24 +384,41 @@
 
         lax.fori_loop(0, 32 // GROUP, group, 0)
 
-    def rest_pass(part, j):
-        s_ref, x_ref, acc_ref, p_ref = parts[part]
+    def load(part, target):
+        acc_ref = parts[part][2]
+        return tuple(
+            tuple(acc_ref[target + t, h, :, to : to + n] for h in range(2) for _, to, n in PIECES[part])
+            for t in range(GROUP)
+        )
+
+    def block_pass(part, block):
+        s_ref, x_ref, acc_ref, _ = parts[part]
+        k = len(PIECES[part])
+
+        def group(i, carry):
+            j, g = lax.div(i, 2), lax.rem(i, 2) * GROUP
+            acc = add_pairs(
+                part, index_ref, table_ref, s_ref, x_ref, block, reduce_member(core, x, z, j) * 8 + g, load(part, j * 8 + g)
+            )
+            for t in range(GROUP):
+                for p, (_, to, n) in enumerate(PIECES[part]):
+                    acc_ref[j * 8 + g + t, 0, :, to : to + n] = acc[t][p]
+                    acc_ref[j * 8 + g + t, 1, :, to : to + n] = acc[t][k + p]
+            return carry
+
+        lax.fori_loop(0, 32 // GROUP, group, 0)
+
+    def last_pass(part, j, blocks):
+        s_ref, x_ref, _, p_ref = parts[part]
         k = len(PIECES[part])
 
         def group(i, carry):
             g = i * GROUP
-            acc = tuple(
-                tuple(acc_ref[j * 8 + g + t, h, :, to : to + n] for h in range(2) for _, to, n in PIECES[part])
-                for t in range(GROUP)
-            )
-
-            def block(r, acc):
-                return add_pairs(
-                    part, index_ref, table_ref, s_ref, x_ref, lax.rem(source_me + r, 4),
-                    reduce_member(core, x, z, j) * 8 + g, acc,
+            acc = load(part, j * 8 + g)
+            for block in blocks:
+                acc = add_pairs(
+                    part, index_ref, table_ref, s_ref, x_ref, block, reduce_member(core, x, z, j) * 8 + g, acc
                 )
-
-            acc = lax.fori_loop(1, 4, block, acc)
             for t in range(GROUP):
                 for p, (_, to, n) in enumerate(PIECES[part]):
                     a, b = acc[t][p], acc[t][k + p]
@@ -420,26 +444,31 @@
     swap(sb_ref, xb_ref, source_me)
     own_pass(1)
 
-    def gathered(part, gathers):
-        for copy in gathers:
-            copy.wait_recv()
-        for r in range(1, 4):
-            swap(parts[part][0], parts[part][1], source_blocks[r])
+    def gathered(part, copy, r):
+        copy.wait_recv()
+        swap(parts[part][0], parts[part][1], source_blocks[r])
 
     def reduce_to(part, r, got_ref):
         block = parts[part][3].at[pl.ds(target_blocks[r] * 8, 8)]
         return send(8 + 3 * part + r - 1, block, got_ref.at[r - 1], target_peers[r - 1])
 
-    gathered(0, gather_a)
-    for r in range(4):
-        rest_pass(0, target_blocks[r])
-    gathered(1, gather_b)
+    for r in (3, 2, 1):
+        gathered(0, gather_a[r - 1], r)
+    for r in (1, 2):
+        last_pass(0, target_blocks[r], source_blocks[1:])
+    for r in (3, 2):
+        gathered(1, gather_b[r - 1], r)
+        block_pass(1, source_blocks[r])
+    gathered(1, gather_b[0], 1)
     reduces_b = []
-    for r in range(1, 4):
-        rest_pass(1, target_blocks[r])
+    for r in (1, 2, 3):
+        last_pass(1, target_blocks[r], source_blocks[1:2])
         reduces_b.append(reduce_to(1, r, gotb_ref))
-    reduces = [reduce_to(0, r, gota_ref) for r in range(1, 4)] + reduces_b
-    rest_pass(1, target_blocks[0])
+    reduces = [reduce_to(0, r, gota_ref) for r in (1, 2)]
+    last_pass(0, target_blocks[3], source_blocks[1:])
+    reduces += [reduce_to(0, 3, gota_ref), *reduces_b]
+    last_pass(1, target_blocks[0], source_blocks[1:2])
+    last_pass(0, target_blocks[0], source_blocks[1:])
 
     def total(part, got_ref):
         p_ref = parts[part][3]
@@ -484,7 +513,7 @@
 
     for n in range(6):
         v = split(jnp.concatenate(to_child(r_ref[16 * n : 16 * n + 16].reshape(128, 384)), axis=0))
-        out_ref[128 * n : 128 * n + 128, :] = dot3((left2_ref[0], left2_ref[1]), v)
+        out_ref[128 * n : 128 * n + 128, :] = dot2(left2_ref[...], v)
     hot_parent, hot_octant = one_hot(parent_ref[...], 8), one_hot(octants_ref[...], 8)
     shifts = [pick(hot_octant, [edge_ref[e, t] for t in range(6)]) for e in range(2)]
     for copy in (forward, backward, *gather_a, *gather_b, *reduces):
@@ -510,6 +539,16 @@
                     )
 
 
+def finish_kernel(in_ref, out_ref, sem):
+    copies = [
+        pltpu.make_async_copy(in_ref.at[pl.ds(96 * n, 96)], out_ref.at[pl.ds(96 * n, 96)], sem.at[n]) for n in range(8)
+    ]
+    for copy in copies:
+        copy.start()
+    for copy in copies:
+        copy.wait()
+
+
 VMEM_SPEC = pl.BlockSpec(memory_space=pltpu.VMEM)
 HBM_SPEC = pl.BlockSpec(memory_space=pltpu.HBM)
 LIMIT = 63 * 2**20
@@ -532,8 +571,8 @@
         out_specs=VMEM_SPEC,
         scratch_shapes=[
             ints((1, KIDS)), ints((1, KIDS)), scalars((1, KIDS)), scalars((1, KIDS)), vm((KIDS, 2, 8, 128)),
-            ints((56, 128)), ints((56, 128)), ints((1, 128)), bf16((OFFSETS + 1, 2, 2304)), bf16((2, 256, 128)),
-            bf16((2, 256, 384)), vm((144, 128)), bf16((2, 2, 256, 128)), bf16((2, 128, 256)), vm((2, 6, 8, 128)),
+            ints((56, 128)), ints((56, 128)), ints((1, 128)), bf16((OFFSETS + 1, 2, 2304)), bf16((256, 128)),
+            bf16((2, 256, 384)), vm((144, 128)), bf16((2, 2, 256, 128)), bf16((128, 256)), vm((2, 6, 8, 128)),
             ints((32, 128)), scalars((32, 128)), ints((8, 128)), scalars((8, 128)),
             bf16((2, 768, 256)), vm((2 * KIDS + 2, 8, 384)), vm((48, 8, 128)), vm((8 * TILES, 128)), vm((TILES, 8, 128)),
             vm((2 * KIDS, 8, 384)), vm((4, TILES, 128)), vm((4, TILES, 128)),
@@ -547,6 +586,15 @@
         child_parent, child_octant.reshape(1, KIDS), child, partner_src.T, partner_off.T, partner_count.reshape(1, 128),
         table, up_left, up_right, phases, down_right, down_left,
     )
+    out = pl.pallas_call(
+        finish_kernel,
+        out_shape=f32(KIDS * 16, 128),
+        in_specs=[HBM_SPEC],
+        out_specs=HBM_SPEC,
+        scratch_shapes=[pltpu.SemaphoreType.DMA((8,))],
+        compiler_params=pltpu.CompilerParams(vmem_limit_bytes=LIMIT),
+        name="finish",
+    )(out)
     return out.reshape(KIDS, 2, 8, 128)
 
 

time: 39 us -> 50.8 us (1.30)
  the two profiles are of different devices: /device:TPU:1 before, /device:TPU:4 now
where the time goes in v5:
time: 50.8 us; the launch traced here: 50.7 us
  Pallas kernels  50.6 us (100%)
    pallas_call x1, Pallas kernels, on_device(): pl.pallas_call(middle_kernel, out_shape=f32(KIDS * 16, 128), in_specs=[HB...  37.6 us
    pallas_call x1, Pallas kernels, on_device(): pl.pallas_call(finish_kernel, out_shape=f32(KIDS * 16, 128), in_specs=[HB...  13.1 us

profile of v5, /device:TPU:4, one launch (start us, length us, event | category | flops | bytes accessed | tf_op | source)
XLA Modules:
  0.0 50.7 jit_solution(14398516803048401418)
XLA Ops:
  0.0 37.6 %middle.1.in_ref = f32[768,128]{1,0:T(8,128)} custom-call(s32[1,48]{1,0:T(1,128)} %parent_hbm.1, s32[1,48]{1,0:T(1,128)} %bitcast.7, f32[48,2,8,128]{3,2,1,0:T(8,128)} %child_hbm.1, s32[56,128]{1,0:T(8,128)} %bitcast.5, s32[56,128]{1,0:T(8,128)} %bitcast.6, s32[1,128]{1,0:T(1,128)} %bitcast.8, bf16[316,2,2304]{2,1,0:T(2,128)(2,1)} %table_hbm.1, ...), custom_call_target="tpu_custom_call" | custom-call | tf_op jit(solution)/shard_map/middle/pallas_call | solution.py:567
  37.6 13.1 %finish.1 = f32[768,128]{1,0:T(8,128)} custom-call(f32[768,128]{1,0:T(8,128)} %middle.1.in_ref), custom_call_target="tpu_custom_call" | custom-call | tf_op jit(solution)/shard_map/finish/pallas_call | solution.py:589

commit v6 on v5

--- a/solution.py
+++ b/solution.py
@@ -260,8 +260,8 @@
     out_ref,
     parent_ref, octants_ref, parents_ref, octant_ref, child_ref, src_ref, off_ref, count_ref, table_ref, left_ref,
     right_ref, base_ref, right2_ref, left2_ref, edge_ref,
-    key_ref, index_ref, kids_ref, kid_ref, y_ref, z_ref, phase_ref, tile_ref, inc_ref, r_ref, pack_ref, halo_ref,
-    sa_ref, sb_ref, xa_ref, xb_ref, acca_ref, accb_ref, pa_ref, pb_ref, gota_ref, gotb_ref, sum_ref,
+    key_ref, index_ref, kids_ref, kid_ref, y_ref, z_ref, phase_ref, tile_ref, inc_ref, r_ref, v_ref, pack_ref, halo_ref,
+    sa_ref, sb_ref, xa_ref, xb_ref, acca_ref, accb_ref, pa_ref, pb_ref, gota_ref, pu_ref, gotu_ref, goto_ref, su_ref, sum_ref,
     local_sem, send_sem, recv_sem,
 ):
     clus, direction, core, x, z = position()
@@ -460,34 +460,99 @@
         gathered(1, gather_b[r - 1], r)
         block_pass(1, source_blocks[r])
     gathered(1, gather_b[0], 1)
-    reduces_b = []
+    low = lax.broadcasted_iota(jnp.int32, (2, 128), 1) < 64
+    for_before, for_after = 2 * core, 2 - 2 * core
+
+    def pack(j):
+        def parent(g, carry):
+            t = j * 8 + g
+            p = [pb_ref[t, :, 128 * n : 128 * n + 128] for n in range(9)]
+            chunks = (
+                (for_before, (p[3], jnp.where(low, p[4], p[1]), p[2])),
+                (1, (p[0], jnp.where(low, p[1], p[4]), p[5])),
+                (for_after, p[6:9]),
+            )
+            for chunk, tiles in chunks:
+                for c in range(3):
+                    pu_ref[chunk, t, :, 128 * c : 128 * c + 128] = tiles[c]
+            return carry
+
+        lax.fori_loop(0, PAR, parent, 0, unroll=2)
+
+    urgent = []
     for r in (1, 2, 3):
         last_pass(1, target_blocks[r], source_blocks[1:2])
-        reduces_b.append(reduce_to(1, r, gotb_ref))
+        pack(target_blocks[r])
+        chunk = pu_ref.at[0, pl.ds(target_blocks[r] * 8, 8)]
+        urgent.append(send(10 + r, chunk, gotu_ref.at[r - 1], target_peers[r - 1]))
+    others = []
+    for r in (1, 2, 3):
+        chunks = pu_ref.at[pl.ds(1, 2), pl.ds(target_blocks[r] * 8, 8)]
+        others.append(send(15 + r, chunks, goto_ref.at[r - 1], target_peers[r - 1]))
     reduces = [reduce_to(0, r, gota_ref) for r in (1, 2)]
     last_pass(0, target_blocks[3], source_blocks[1:])
-    reduces += [reduce_to(0, 3, gota_ref), *reduces_b]
+    reduces.append(reduce_to(0, 3, gota_ref))
     last_pass(1, target_blocks[0], source_blocks[1:2])
+    pack(target_blocks[0])
     last_pass(0, target_blocks[0], source_blocks[1:])
 
-    def total(part, got_ref):
-        p_ref = parts[part][3]
-        for copy in reduces[3 * part : 3 * part + 3]:
-            copy.wait_recv()
-
+    def to_rows(chunk, slot):
         def parent(g, carry):
-            sum_ref[g] = (p_ref[target_me * 8 + g] + got_ref[0, g]) + (got_ref[1, g] + got_ref[2, g])
+            for c in range(3):
+                pack_ref[slot, pl.ds(g * 6 + c, 2, stride=3), :] = su_ref[chunk, g, :, 128 * c : 128 * c + 128]
             return carry
 
-        lax.fori_loop(0, PAR, parent, 0)
-        unrelay(sum_ref, tile_ref, part)
-
-    total(1, gotb_ref)
-    pack_ref[2] = jnp.where(even, tile_ref[at2, :], tile_ref[at1, :])
-    last_back = send(14, pack_ref.at[2], halo_ref.at[2], before)
-    pack_ref[3] = tile_ref[at6, :]
-    last_on = send(15, pack_ref.at[3], halo_ref.at[3], after)
-    total(0, gota_ref)
+        lax.fori_loop(0, PAR, parent, 0, unroll=2)
+
+    for copy in urgent:
+        copy.wait_recv()
+
+    def first_total(g, carry):
+        su_ref[0, g] = (pu_ref[0, target_me * 8 + g] + gotu_ref[0, g]) + (gotu_ref[1, g] + gotu_ref[2, g])
+        return carry
+
+    lax.fori_loop(0, PAR, first_total, 0, unroll=2)
+    to_rows(0, 2)
+    far = (clus, lax.rem(direction + N_DIR - 1 + 2 * core, N_DIR))
+    near = (clus, direction + 1 - 2 * core)
+    last_far = send(14, pack_ref.at[2], halo_ref.at[2 + core], far)
+    for copy in others:
+        copy.wait_recv()
+
+    def other_totals(g, carry):
+        for n in range(2):
+            own_sum = pu_ref[1 + n, target_me * 8 + g]
+            su_ref[1 + n, g] = (own_sum + goto_ref[0, n, g]) + (goto_ref[1, n, g] + goto_ref[2, n, g])
+        return carry
+
+    lax.fori_loop(0, PAR, other_totals, 0, unroll=2)
+    to_rows(2, 3)
+    last_near = send(15, pack_ref.at[3], halo_ref.at[3 - core], near)
+
+    def unpack(g, carry):
+        f, rest, last = (
+            [su_ref[chunk, g, :, 128 * c : 128 * c + 128] for c in range(3)] for chunk in (for_before, 1, for_after)
+        )
+        pairs = (
+            (0, (rest[0], jnp.where(low, rest[1], f[1]), f[2])),
+            (1, (f[0], jnp.where(low, f[1], rest[1]), rest[2])),
+            (5, last),
+        )
+        for q, tiles in pairs:
+            for c in range(3):
+                tile_ref[pl.ds((g * 6 + c) * 8 + q + 1, 2, stride=24), :] = tiles[c]
+        return carry
+
+    lax.fori_loop(0, PAR, unpack, 0)
+    for copy in reduces:
+        copy.wait_recv()
+
+    def last_total(g, carry):
+        sum_ref[g] = (pa_ref[target_me * 8 + g] + gota_ref[0, g]) + (gota_ref[1, g] + gota_ref[2, g])
+        return carry
+
+    lax.fori_loop(0, PAR, last_total, 0, unroll=2)
+    unrelay(sum_ref, tile_ref, 0)
     pair = lax.broadcasted_iota(jnp.int32, (8, 128), 0)
     inside = (pair > 0) & (pair < 7)
     for t in range(TILES):
@@ -511,15 +576,16 @@
             dot3((hi[:, 128:], lo[:, 128:]), (right2_ref[0, 1], right2_ref[1, 1])),
         )
 
+    v_ref[0], v_ref[1] = to_child(r_ref[...].reshape(768, 384))
     for n in range(6):
-        v = split(jnp.concatenate(to_child(r_ref[16 * n : 16 * n + 16].reshape(128, 384)), axis=0))
-        out_ref[128 * n : 128 * n + 128, :] = dot2(left2_ref[...], v)
+        at = slice(128 * n, 128 * n + 128)
+        out_ref[at, :] = dot2(left2_ref[...], split(jnp.concatenate([v_ref[0, at, :], v_ref[1, at, :]], axis=0)))
     hot_parent, hot_octant = one_hot(parent_ref[...], 8), one_hot(octants_ref[...], 8)
     shifts = [pick(hot_octant, [edge_ref[e, t] for t in range(6)]) for e in range(2)]
-    for copy in (forward, backward, *gather_a, *gather_b, *reduces):
+    for copy in (forward, backward, *gather_a, *gather_b, *reduces, *urgent, *others):
         copy.wait_send()
-    last_back.wait()
-    last_on.wait()
+    last_near.wait()
+    last_far.wait()
     rows = []
     for e in range(2):
         values = pick(hot_parent, [halo_ref[3 - e, pl.ds(t, 8, stride=6), :] for t in range(6)])
@@ -539,16 +605,6 @@
                     )
 
 
-def finish_kernel(in_ref, out_ref, sem):
-    copies = [
-        pltpu.make_async_copy(in_ref.at[pl.ds(96 * n, 96)], out_ref.at[pl.ds(96 * n, 96)], sem.at[n]) for n in range(8)
-    ]
-    for copy in copies:
-        copy.start()
-    for copy in copies:
-        copy.wait()
-
-
 VMEM_SPEC = pl.BlockSpec(memory_space=pltpu.VMEM)
 HBM_SPEC = pl.BlockSpec(memory_space=pltpu.HBM)
 LIMIT = 63 * 2**20
@@ -575,10 +631,11 @@
             bf16((2, 256, 384)), vm((144, 128)), bf16((2, 2, 256, 128)), bf16((128, 256)), vm((2, 6, 8, 128)),
             ints((32, 128)), scalars((32, 128)), ints((8, 128)), scalars((8, 128)),
             bf16((2, 768, 256)), vm((2 * KIDS + 2, 8, 384)), vm((48, 8, 128)), vm((8 * TILES, 128)), vm((TILES, 8, 128)),
-            vm((2 * KIDS, 8, 384)), vm((4, TILES, 128)), vm((4, TILES, 128)),
+            vm((2 * KIDS, 8, 384)), vm((2, 768, 128)), vm((4, TILES, 128)), vm((4, TILES, 128)),
             *[vm((32, 2, HALF))] * 4, *[vm((32, 2, 2, HALF))] * 2, *[vm((32, 2, HALF))] * 2,
-            *[vm((3, 8, 2, HALF))] * 2, vm((8, 2, HALF)),
-            pltpu.SemaphoreType.DMA((14,)), pltpu.SemaphoreType.DMA((16,)), pltpu.SemaphoreType.DMA((16,)),
+            vm((3, 8, 2, HALF)), vm((3, 32, 2, 384)), vm((3, 8, 2, 384)), vm((3, 2, 8, 2, 384)), vm((3, 8, 2, 384)),
+            vm((8, 2, HALF)),
+            pltpu.SemaphoreType.DMA((14,)), pltpu.SemaphoreType.DMA((19,)), pltpu.SemaphoreType.DMA((19,)),
         ],
         compiler_params=pltpu.CompilerParams(collective_id=0, has_side_effects=True, vmem_limit_bytes=LIMIT),
         name="middle",
@@ -586,15 +643,6 @@
         child_parent, child_octant.reshape(1, KIDS), child, partner_src.T, partner_off.T, partner_count.reshape(1, 128),
         table, up_left, up_right, phases, down_right, down_left,
     )
-    out = pl.pallas_call(
-        finish_kernel,
-        out_shape=f32(KIDS * 16, 128),
-        in_specs=[HBM_SPEC],
-        out_specs=HBM_SPEC,
-        scratch_shapes=[pltpu.SemaphoreType.DMA((8,))],
-        compiler_params=pltpu.CompilerParams(vmem_limit_bytes=LIMIT),
-        name="finish",
-    )(out)
     return out.reshape(KIDS, 2, 8, 128)
 
 

time: 50.8 us -> 39.1 us (0.77)
  Pallas kernels: 50.6 us -> 37.1 us
  local copies, waits for them, and re-layouts: 0 us -> 1.77 us
    pallas_call x1 -> x0, Pallas kernels: 13.1 us -> none  [on_device(): pl.pallas_call(finish_kernel, out_shape=f32(KIDS * 16, 128), in_specs=[HB...]
    unnamed x0 -> x1, local copies, waits for them, and re-layouts: none -> 1.77 us
where the time goes in v6:
time: 39.1 us; the launch traced here: 38.9 us
  Pallas kernels  37.1 us (95%)
  local copies, waits for them, and re-layouts  1.77 us (5%)
    pallas_call x1, Pallas kernels, on_device(): pl.pallas_call(middle_kernel, out_shape=f32(KIDS * 16, 128), in_specs=[HB...  37.1 us
    unnamed x1, local copies, waits for them, and re-layouts  1.77 us

profile of v6, /device:TPU:4, one launch (start us, length us, event | category | flops | bytes accessed | tf_op | source)
XLA Modules:
  0.0 38.9 jit_solution(15075452778295451749)
XLA Ops:
  0.0 37.1 %middle.1 = f32[768,128]{1,0:T(8,128)} custom-call(s32[1,48]{1,0:T(1,128)} %parent_hbm.1, s32[1,48]{1,0:T(1,128)} %bitcast.8, f32[48,2,8,128]{3,2,1,0:T(8,128)} %child_hbm.1, s32[56,128]{1,0:T(8,128)} %bitcast.6, s32[56,128]{1,0:T(8,128)} %bitcast.7, s32[1,128]{1,0:T(1,128)} %bitcast.9, bf16[316,2,2304]{2,1,0:T(2,128)(2,1)} %table_hbm.1, ...), custom_call_target="tpu_custom_call" | custom-call | tf_op jit(solution)/shard_map/middle/pallas_call | solution.py:623
  37.1 1.8 %copy.14 = f32[48,2,8,128]{3,2,1,0:T(8,128)} copy(f32[48,2,8,128]{3,2,1,0:T(8,128)} %bitcast.5) | data formatting | bytes 786432

commit v7 on v6

--- a/solution.py
+++ b/solution.py
@@ -204,9 +204,9 @@
 HALF = 1152
 
 
-def relay(tile_ref, s_ref, part, first):
+def relay(tile_ref, s_ref, part, first, places=(0, 1, 2)):
     def parent(g, carry):
-        for n, q in enumerate(PAIRS[part]):
+        for n, q in ((n, PAIRS[part][n]) for n in places):
             for c in range(3):
                 lanes = slice(128 * (3 * n + c), 128 * (3 * n + c) + 128)
                 s_ref[first + g, :, lanes] = tile_ref[pl.ds((g * 6 + c) * 8 + q + 1, 2, stride=24), :]
@@ -428,24 +428,64 @@
 
         lax.fori_loop(0, PAR // GROUP, group, 0)
 
-    own_pass(0)
-
     even = even_lanes()
-    forward.wait_recv()
-    got = halo_ref[0]
-    at1, at2, at6 = (pl.ds(s, TILES, stride=8) for s in (1, 2, 6))
-    tile_ref[at1, :] = tile_ref[at1, :] + jnp.where(even, 0.0, got)
-    tile_ref[at2, :] = tile_ref[at2, :] + jnp.where(even, got, 0.0)
-    backward.wait_recv()
-    tile_ref[at6, :] = tile_ref[at6, :] + halo_ref[1]
-    relay(tile_ref, sb_ref, 1, own)
-    block_b = sb_ref.at[pl.ds(own, 8)]
-    gather_b = [send(5 + r, block_b, block_b, peer) for r, peer in enumerate(source_peers)]
+    at1, at2, at6 = (pl.ds(pair, TILES, stride=8) for pair in (1, 2, 6))
+
+    def from_before():
+        forward.wait_recv()
+        got = halo_ref[0]
+        tile_ref[at1, :] = tile_ref[at1, :] + jnp.where(even, 0.0, got)
+        tile_ref[at2, :] = tile_ref[at2, :] + jnp.where(even, got, 0.0)
+        relay(tile_ref, sb_ref, 1, own, (0, 1))
+
+    def from_after():
+        backward.wait_recv()
+        tile_ref[at6, :] = tile_ref[at6, :] + halo_ref[1]
+        relay(tile_ref, sb_ref, 1, own, (2,))
+
+    def b_copy(first, lanes, late, r):
+        n = (19 if late else 5) + r - 1
+        block = sb_ref.at[pl.ds(own, 8), :, pl.ds(first, lanes)]
+        return pltpu.make_async_remote_copy(
+            block, block, send_sem.at[n], recv_sem.at[n], device_id=source_peers[r - 1], device_id_type=MESH
+        )
+
+    def b_wait(r, send_side):
+        for c in range(2):
+
+            @pl.when(core == c)
+            def _():
+                for first, lanes, late in ((0, 768, c == 0), (768, 384, c == 1)):
+                    copy = b_copy(first, lanes, late, r)
+                    if send_side:
+                        copy.wait_send()
+                    else:
+                        copy.wait_recv()
+
+    for late in (False, True):
+
+        @pl.when(core == int(late))
+        def _(late=late):
+            from_after()
+            for r in (1, 2, 3):
+                b_copy(768, 384, late, r).start()
+
+        @pl.when(core == 1 - int(late))
+        def _(late=late):
+            from_before()
+            for r in (1, 2, 3):
+                b_copy(0, 768, late, r).start()
+
+        if not late:
+            own_pass(0)
     swap(sb_ref, xb_ref, source_me)
     own_pass(1)
 
-    def gathered(part, copy, r):
-        copy.wait_recv()
+    def gathered(part, r):
+        if part == 0:
+            gather_a[r - 1].wait_recv()
+        else:
+            b_wait(r, False)
         swap(parts[part][0], parts[part][1], source_blocks[r])
 
     def reduce_to(part, r, got_ref):
@@ -453,13 +493,13 @@
         return send(8 + 3 * part + r - 1, block, got_ref.at[r - 1], target_peers[r - 1])
 
     for r in (3, 2, 1):
-        gathered(0, gather_a[r - 1], r)
+        gathered(0, r)
     for r in (1, 2):
         last_pass(0, target_blocks[r], source_blocks[1:])
     for r in (3, 2):
-        gathered(1, gather_b[r - 1], r)
+        gathered(1, r)
         block_pass(1, source_blocks[r])
-    gathered(1, gather_b[0], 1)
+    gathered(1, 1)
     low = lax.broadcasted_iota(jnp.int32, (2, 128), 1) < 64
     for_before, for_after = 2 * core, 2 - 2 * core
 
@@ -582,8 +622,10 @@
         out_ref[at, :] = dot2(left2_ref[...], split(jnp.concatenate([v_ref[0, at, :], v_ref[1, at, :]], axis=0)))
     hot_parent, hot_octant = one_hot(parent_ref[...], 8), one_hot(octants_ref[...], 8)
     shifts = [pick(hot_octant, [edge_ref[e, t] for t in range(6)]) for e in range(2)]
-    for copy in (forward, backward, *gather_a, *gather_b, *reduces, *urgent, *others):
+    for copy in (forward, backward, *gather_a, *reduces, *urgent, *others):
         copy.wait_send()
+    for r in (1, 2, 3):
+        b_wait(r, True)
     last_near.wait()
     last_far.wait()
     rows = []
@@ -635,7 +677,7 @@
             *[vm((32, 2, HALF))] * 4, *[vm((32, 2, 2, HALF))] * 2, *[vm((32, 2, HALF))] * 2,
             vm((3, 8, 2, HALF)), vm((3, 32, 2, 384)), vm((3, 8, 2, 384)), vm((3, 2, 8, 2, 384)), vm((3, 8, 2, 384)),
             vm((8, 2, HALF)),
-            pltpu.SemaphoreType.DMA((14,)), pltpu.SemaphoreType.DMA((19,)), pltpu.SemaphoreType.DMA((19,)),
+            pltpu.SemaphoreType.DMA((14,)), pltpu.SemaphoreType.DMA((22,)), pltpu.SemaphoreType.DMA((22,)),
         ],
         compiler_params=pltpu.CompilerParams(collective_id=0, has_side_effects=True, vmem_limit_bytes=LIMIT),
         name="middle",

time: 39.1 us -> 38.7 us (0.990)
  the two profiles are of different devices: /device:TPU:4 before, /device:TPU:1 now
where the time goes in v7:
time: 38.7 us; the launch traced here: 38.1 us
  Pallas kernels  36.3 us (94%)
  local copies, waits for them, and re-layouts  1.77 us (5%)
    pallas_call x1, Pallas kernels, on_device(): pl.pallas_call(middle_kernel, out_shape=f32(KIDS * 16, 128), in_specs=[HB...  36.3 us
    unnamed x1, local copies, waits for them, and re-layouts  1.77 us

profile of v7, /device:TPU:1, one launch (start us, length us, event | category | flops | bytes accessed | tf_op | source)
XLA Modules:
  0.0 38.1 jit_solution(16962226415979263493)
XLA Ops:
  0.0 36.3 %middle.1 = f32[768,128]{1,0:T(8,128)} custom-call(s32[1,48]{1,0:T(1,128)} %parent_hbm.1, s32[1,48]{1,0:T(1,128)} %bitcast.8, f32[48,2,8,128]{3,2,1,0:T(8,128)} %child_hbm.1, s32[56,128]{1,0:T(8,128)} %bitcast.6, s32[56,128]{1,0:T(8,128)} %bitcast.7, s32[1,128]{1,0:T(1,128)} %bitcast.9, bf16[316,2,2304]{2,1,0:T(2,128)(2,1)} %table_hbm.1, ...), custom_call_target="tpu_custom_call" | custom-call | tf_op jit(solution)/shard_map/middle/pallas_call | solution.py:665
  36.4 1.8 %copy.14 = f32[48,2,8,128]{3,2,1,0:T(8,128)} copy(f32[48,2,8,128]{3,2,1,0:T(8,128)} %bitcast.5) | data formatting | bytes 786432

commit v8 on v7

--- a/solution.py
+++ b/solution.py
@@ -492,10 +492,6 @@
         block = parts[part][3].at[pl.ds(target_blocks[r] * 8, 8)]
         return send(8 + 3 * part + r - 1, block, got_ref.at[r - 1], target_peers[r - 1])
 
-    for r in (3, 2, 1):
-        gathered(0, r)
-    for r in (1, 2):
-        last_pass(0, target_blocks[r], source_blocks[1:])
     for r in (3, 2):
         gathered(1, r)
         block_pass(1, source_blocks[r])
@@ -529,9 +525,12 @@
     for r in (1, 2, 3):
         chunks = pu_ref.at[pl.ds(1, 2), pl.ds(target_blocks[r] * 8, 8)]
         others.append(send(15 + r, chunks, goto_ref.at[r - 1], target_peers[r - 1]))
-    reduces = [reduce_to(0, r, gota_ref) for r in (1, 2)]
-    last_pass(0, target_blocks[3], source_blocks[1:])
-    reduces.append(reduce_to(0, 3, gota_ref))
+    for r in (3, 2, 1):
+        gathered(0, r)
+    reduces = []
+    for r in (1, 2, 3):
+        last_pass(0, target_blocks[r], source_blocks[1:])
+        reduces.append(reduce_to(0, r, gota_ref))
     last_pass(1, target_blocks[0], source_blocks[1:2])
     pack(target_blocks[0])
     last_pass(0, target_blocks[0], source_blocks[1:])

time: 38.7 us -> 38.7 us (level)
  no operation moved by 1% of the time
where the time goes in v8:
time: 38.7 us; the launch traced here: 38.1 us
  Pallas kernels  36.3 us (94%)
  local copies, waits for them, and re-layouts  1.77 us (5%)
    pallas_call x1, Pallas kernels, on_device(): pl.pallas_call(middle_kernel, out_shape=f32(KIDS * 16, 128), in_specs=[HB...  36.3 us
    unnamed x1, local copies, waits for them, and re-layouts  1.77 us

profile of v8, /device:TPU:1, one launch (start us, length us, event | category | flops | bytes accessed | tf_op | source)
XLA Modules:
  0.0 38.1 jit_solution(12033424418897961856)
XLA Ops:
  0.0 36.3 %middle.1 = f32[768,128]{1,0:T(8,128)} custom-call(s32[1,48]{1,0:T(1,128)} %parent_hbm.1, s32[1,48]{1,0:T(1,128)} %bitcast.8, f32[48,2,8,128]{3,2,1,0:T(8,128)} %child_hbm.1, s32[56,128]{1,0:T(8,128)} %bitcast.6, s32[56,128]{1,0:T(8,128)} %bitcast.7, s32[1,128]{1,0:T(1,128)} %bitcast.9, bf16[316,2,2304]{2,1,0:T(2,128)(2,1)} %table_hbm.1, ...), custom_call_target="tpu_custom_call" | custom-call | tf_op jit(solution)/shard_map/middle/pallas_call | solution.py:664
  36.4 1.8 %copy.14 = f32[48,2,8,128]{3,2,1,0:T(8,128)} copy(f32[48,2,8,128]{3,2,1,0:T(8,128)} %bitcast.5) | data formatting | bytes 786432

commit v9 on v8

--- a/solution.py
+++ b/solution.py
@@ -533,7 +533,6 @@
         reduces.append(reduce_to(0, r, gota_ref))
     last_pass(1, target_blocks[0], source_blocks[1:2])
     pack(target_blocks[0])
-    last_pass(0, target_blocks[0], source_blocks[1:])
 
     def to_rows(chunk, slot):
         def parent(g, carry):
@@ -555,6 +554,7 @@
     far = (clus, lax.rem(direction + N_DIR - 1 + 2 * core, N_DIR))
     near = (clus, direction + 1 - 2 * core)
     last_far = send(14, pack_ref.at[2], halo_ref.at[2 + core], far)
+    last_pass(0, target_blocks[0], source_blocks[1:])
     for copy in others:
         copy.wait_recv()
 

time: 38.7 us -> 38.7 us (level)
  no operation moved by 1% of the time
where the time goes in v9:
time: 38.7 us; the launch traced here: 38.1 us
  Pallas kernels  36.4 us (94%)
  local copies, waits for them, and re-layouts  1.77 us (5%)
    pallas_call x1, Pallas kernels, on_device(): pl.pallas_call(middle_kernel, out_shape=f32(KIDS * 16, 128), in_specs=[HB...  36.4 us
    unnamed x1, local copies, waits for them, and re-layouts  1.77 us

profile of v9, /device:TPU:1, one launch (start us, length us, event | category | flops | bytes accessed | tf_op | source)
XLA Modules:
  0.0 38.1 jit_solution(10339194418834401903)
XLA Ops:
  0.0 36.4 %middle.1 = f32[768,128]{1,0:T(8,128)} custom-call(s32[1,48]{1,0:T(1,128)} %parent_hbm.1, s32[1,48]{1,0:T(1,128)} %bitcast.8, f32[48,2,8,128]{3,2,1,0:T(8,128)} %child_hbm.1, s32[56,128]{1,0:T(8,128)} %bitcast.6, s32[56,128]{1,0:T(8,128)} %bitcast.7, s32[1,128]{1,0:T(1,128)} %bitcast.9, bf16[316,2,2304]{2,1,0:T(2,128)(2,1)} %table_hbm.1, ...), custom_call_target="tpu_custom_call" | custom-call | tf_op jit(solution)/shard_map/middle/pallas_call | solution.py:664
  36.4 1.8 %copy.14 = f32[48,2,8,128]{3,2,1,0:T(8,128)} copy(f32[48,2,8,128]{3,2,1,0:T(8,128)} %bitcast.5) | data formatting | bytes 786432

commit v10 on v9

--- a/solution.py
+++ b/solution.py
@@ -521,15 +521,17 @@
         pack(target_blocks[r])
         chunk = pu_ref.at[0, pl.ds(target_blocks[r] * 8, 8)]
         urgent.append(send(10 + r, chunk, gotu_ref.at[r - 1], target_peers[r - 1]))
+    for r in (3, 2, 1):
+        gathered(0, r)
+    last_pass(0, target_blocks[1], source_blocks[1:])
     others = []
     for r in (1, 2, 3):
         chunks = pu_ref.at[pl.ds(1, 2), pl.ds(target_blocks[r] * 8, 8)]
         others.append(send(15 + r, chunks, goto_ref.at[r - 1], target_peers[r - 1]))
-    for r in (3, 2, 1):
-        gathered(0, r)
     reduces = []
     for r in (1, 2, 3):
-        last_pass(0, target_blocks[r], source_blocks[1:])
+        if r > 1:
+            last_pass(0, target_blocks[r], source_blocks[1:])
         reduces.append(reduce_to(0, r, gota_ref))
     last_pass(1, target_blocks[0], source_blocks[1:2])
     pack(target_blocks[0])

time: 38.7 us -> 38.9 us (level)
  the two profiles are of different devices: /device:TPU:1 before, /device:TPU:4 now
where the time goes in v10:
time: 38.9 us; the launch traced here: 38.7 us
  Pallas kernels  36.9 us (95%)
  local copies, waits for them, and re-layouts  1.77 us (5%)
    pallas_call x1, Pallas kernels, on_device(): pl.pallas_call(middle_kernel, out_shape=f32(KIDS * 16, 128), in_specs=[HB...  36.9 us
    unnamed x1, local copies, waits for them, and re-layouts  1.77 us

profile of v10, /device:TPU:4, one launch (start us, length us, event | category | flops | bytes accessed | tf_op | source)
XLA Modules:
  0.0 38.7 jit_solution(11647564998863394157)
XLA Ops:
  0.0 36.9 %middle.1 = f32[768,128]{1,0:T(8,128)} custom-call(s32[1,48]{1,0:T(1,128)} %parent_hbm.1, s32[1,48]{1,0:T(1,128)} %bitcast.8, f32[48,2,8,128]{3,2,1,0:T(8,128)} %child_hbm.1, s32[56,128]{1,0:T(8,128)} %bitcast.6, s32[56,128]{1,0:T(8,128)} %bitcast.7, s32[1,128]{1,0:T(1,128)} %bitcast.9, bf16[316,2,2304]{2,1,0:T(2,128)(2,1)} %table_hbm.1, ...), custom_call_target="tpu_custom_call" | custom-call | tf_op jit(solution)/shard_map/middle/pallas_call | solution.py:666
  36.9 1.8 %copy.14 = f32[48,2,8,128]{3,2,1,0:T(8,128)} copy(f32[48,2,8,128]{3,2,1,0:T(8,128)} %bitcast.5) | data formatting | bytes 786432
